TPU v7x, 256 devices: a whole 4x4x8 slice. The times are simulated.
256 devices in a mesh: dp: 4 (over y), latent: 64 (over x, z, core).
Axes of the slice: x: 4, y: 4, z: 8, core: 2. Of those that a mesh axis runs over, the one named last changes fastest.
Arguments:
- acts: bfloat16 [32768, 8192], P(('dp', 'latent')), may hold values from -6 to 6
- blocks: int32 [32768, 2], P(('dp', 'latent')), may hold values from 0 to 191, as said below
- w_enc: bfloat16 [8192, 12288], P(None, 'latent'), may hold values from -0.0625 to 0.0625
- b_enc: float32 [12288], P('latent'), may hold values from -3 to 3
- w_dec: bfloat16 [12288, 8192], P('latent'), may hold values from -0.0625 to 0.0625
- b_dec: float32 [8192], replicated, may hold values from -3 to 3
Outputs:
- grad_w_enc: float32 [8192, 12288], P('dp', 'latent')
- grad_b_enc: float32 [12288], P('latent')
- grad_w_dec: float32 [12288, 8192], P('latent', 'dp')
Inputs may be any that keep to these rules, and one draw needn't show every extreme that they name: Each row names 2 different blocks. Block b lies on index b // 3 of latent. Among the rows of one device no block is named more than 2 times and the blocks of one index of latent are named no more than 6 times in all; in every device some block is named exactly 2 times and some index of latent exactly 6 times.
All inputs are finite; a program needn't handle non-finite values.
Results may differ from a plain program's by a relative error of at most 0.004.
Values may be sent and summed in bfloat16 or wider, within the bound.
A program may use at most 128 MiB of HBM per device.

v0:
```python
import jax
import jax.numpy as jnp
from jax import lax
from jax.sharding import PartitionSpec as P

BW = 64


def gelu_slope(value):
    return (
        0.5 * (1.0 + lax.erf(value * 0.7071067811865476))
        + value * jnp.exp(-0.5 * value * value) * 0.3989422804014327
    )


def shards(acts, blocks, w_enc, b_enc, w_dec, b_dec):
    rows, width = acts.shape
    top = blocks.shape[1]
    owners = lax.axis_size("latent")
    local = w_enc.shape[1] // BW
    nblk = local * owners
    room = max(2, 2 * rows * top // nblk)
    flat = blocks.reshape(-1)
    onehot = (flat[:, None] == jnp.arange(nblk, dtype=jnp.int32)[None, :]).astype(jnp.int32)
    earlier = jnp.cumsum(onehot, axis=0) - onehot
    rank = jnp.sum(earlier * onehot, axis=1)
    target = flat * room + rank
    source_row = jnp.arange(rows * top, dtype=jnp.int32) // top
    padded_total = nblk * room
    w_enc3 = w_enc.reshape(width, local, BW)
    bias3 = b_enc.reshape(local, BW)
    w_dec3 = w_dec.reshape(local, BW, width)

    def dispatch(values):
        filled = jnp.zeros((padded_total, width), jnp.bfloat16).at[target].set(values[source_row])
        return filled.reshape(owners, local, room, width)

    inputs = lax.all_to_all(dispatch(acts), "latent", split_axis=0, concat_axis=0, tiled=True)
    pre = (
        jnp.einsum("sbcd,dbe->sbce", inputs, w_enc3, preferred_element_type=jnp.float32)
        + bias3[None, :, None, :]
    )
    code = jax.nn.gelu(pre, approximate=False).astype(jnp.bfloat16)
    part = jnp.einsum("sbce,bed->sbcd", code, w_dec3, preferred_element_type=jnp.float32).astype(
        jnp.bfloat16
    )
    returned = lax.all_to_all(part, "latent", split_axis=0, concat_axis=0, tiled=True)
    picked = returned.reshape(padded_total, width)[target]
    recon = jnp.sum(picked.astype(jnp.float32).reshape(rows, top, width), axis=1)
    errors = (recon + b_dec - acts.astype(jnp.float32)).astype(jnp.bfloat16)
    wanted = lax.all_to_all(dispatch(errors), "latent", split_axis=0, concat_axis=0, tiled=True)
    g_code = jnp.einsum("sbcd,bed->sbce", wanted, w_dec3, preferred_element_type=jnp.float32)
    g_pre = g_code * gelu_slope(pre)
    g_half = g_pre.astype(jnp.bfloat16)
    bias_term = jnp.sum(g_pre, axis=(0, 2)).reshape(local * BW)
    enc_term = jnp.einsum(
        "sbcd,sbce->dbe", inputs, g_half, preferred_element_type=jnp.float32
    ).reshape(width, local * BW)
    grad_w_enc = lax.psum_scatter(enc_term, "dp", scatter_dimension=0, tiled=True)
    dec_term = jnp.einsum(
        "sbce,sbcd->bed", code, wanted, preferred_element_type=jnp.float32
    ).reshape(local * BW, width)
    grad_w_dec = lax.psum_scatter(dec_term, "dp", scatter_dimension=1, tiled=True)
    grad_b_enc = lax.psum(bias_term, "dp")
    return (grad_w_enc, grad_b_enc, grad_w_dec)


def solution(mesh):
    return jax.shard_map(
        shards,
        mesh=mesh,
        in_specs=(
            P(("dp", "latent"), None),
            P(("dp", "latent"), None),
            P(None, "latent"),
            P("latent"),
            P("latent", None),
            P(),
        ),
        out_specs=(P("dp", "latent"), P("latent"), P("latent", "dp")),
        check_vma=False,
    )
```

profile of v0, /device:TPU:1, one launch (start us, length us, event | category | flops | bytes accessed | tf_op | source)
XLA Modules:
  0.0 760.2 jit_solution(18301273393950844195)
XLA Ops:
  7.2 0.8 broadcast_multiply_fusion
  8.0 0.9 copy.22
  8.9 0.1 eq.29
  9.1 0.1 eq.25
  9.2 0.1 copy.21
  9.3 0.1 mul.57
  9.6 0.2 fusion.27
  9.9 0.7 broadcast_add_fusion
  10.6 1.1 copy.25
  11.7 19.5 %scatter_custom_fusion = bf16[384,8192]{1,0:T(8,128)(2,1)} fusion(s32[256]{0:T(256)S(1)} %bitcast.68, bf16[128,8192]{1,0:T(8,128)(2,1)} %param.6, s32[1024]{0:T(1024)S(1)} %pad_clamp_fusion.1, bf16[]{:T(256)} %constant.39.clone.1), kind=kCustom, calls=%fused_computation.17 | custom fusion | bytes 6291968 | tf_op jit(solution)/shard_map/scatter | solution.py:35
  31.2 10.9 %reshape.126 = bf16[64,3,2,8192]{3,2,1,0:T(2,128)(2,1)} reshape(bf16[384,8192]{1,0:T(8,128)(2,1)} %scatter_custom_fusion) | data formatting | bytes 12582912 | tf_op jit(solution)/shard_map/reshape | solution.py:36
  42.1 13.7 %all-to-all-start = ((bf16[64,3,2,8192]{3,2,1,0:T(2,128)(2,1)}), bf16[64,3,2,8192]{3,2,1,0:T(2,128)(2,1)}, u32[]{:S(2)}, u32[]{:S(2)}) async-start(bf16[64,3,2,8192]{3,2,1,0:T(2,128)(2,1)} %reshape.126), calls=%async_computation | async-start | bytes 12582912 | tf_op jit(solution)/shard_map/all_to_all | solution.py:38
  55.8 140.6 %all-to-all-done = bf16[64,3,2,8192]{3,2,1,0:T(2,128)(2,1)} async-done(((bf16[64,3,2,8192]{3,2,1,0:T(2,128)(2,1)}), bf16[64,3,2,8192]{3,2,1,0:T(2,128)(2,1)}, u32[]{:S(2)}, u32[]{:S(2)}) %all-to-all-start) | async-done | bytes 6291488 | tf_op jit(solution)/shard_map/all_to_all | solution.py:38
  196.4 11.0 %fusion.24 = f32[64,3,2,64]{3,0,2,1:T(8,128)S(1)} fusion(bf16[8192,3,64,1]{0,2,3,1:T(8,128)(2,1)} %bitcast.72, bf16[64,3,2,8192]{3,2,1,0:T(2,128)(2,1)} %all-to-all-done, f32[3,64]{1,0:T(4,128)S(1)} %add.79), kind=kOutput, calls=%fused_computation.25 | convolution fusion | flops 402677760 | bytes 9536256 | tf_op jit(solution)/shard_map/sbcd,dbe->sbce/dot_general | solution.py:40
  207.4 2.1 fusion
  209.5 15.4 %copy.27 = bf16[64,3,2,8192]{3,2,1,0:T(2,128)(2,1)} copy(bf16[64,3,2,8192]{3,0,2,1:T(8,128)(2,1)S(1)} %fusion) | data formatting | bytes 12582912 | tf_op jit(solution)/shard_map/convert_element_type | solution.py:44
  224.9 6.0 all-to-all-start.1
  230.9 140.8 %all-to-all-done.1 = bf16[64,3,2,8192]{3,2,1,0:T(2,128)(2,1)} async-done(((bf16[64,3,2,8192]{3,2,1,0:T(2,128)(2,1)}), bf16[64,3,2,8192]{3,2,1,0:T(2,128)(2,1)}, u32[]{:S(2)}, u32[]{:S(2)}) %all-to-all-start.1) | async-done | bytes 6291488 | tf_op jit(solution)/shard_map/all_to_all | solution.py:47
  371.7 10.5 %reshape.129 = bf16[384,8192]{1,0:T(8,128)(2,1)} reshape(bf16[64,3,2,8192]{3,2,1,0:T(2,128)(2,1)} %all-to-all-done.1) | data formatting | bytes 12582912 | tf_op jit(solution)/shard_map/reshape | solution.py:48
  382.2 12.6 %gather_fusion = bf16[256,8192]{1,0:T(8,128)(2,1)} fusion(bf16[384,8192]{1,0:T(8,128)(2,1)} %reshape.129, s32[1024]{0:T(1024)S(1)} %pad_clamp_fusion), kind=kCustom, calls=%fused_computation.1 | custom fusion | bytes 8389632 | tf_op jit(solution)/shard_map/gather | solution.py:48
  394.8 9.7 %reshape.134 = f32[128,2,8192]{2,1,0:T(2,128)} reshape(bf16[256,8192]{1,0:T(8,128)(2,1)} %gather_fusion) | data formatting | bytes 12582912 | tf_op jit(solution)/shard_map/convert_element_type | solution.py:49
  404.5 13.5 %reduce_sum.31 = f32[128,8192]{1,0:T(8,128)} reduce(f32[128,2,8192]{2,1,0:T(2,128)} %reshape.134, f32[]{:T(128)} %constant.26.clone.1), dimensions={1}, to_apply=%region_4.5 | reduce | flops 1048576 | bytes 12582916 | tf_op jit(solution)/shard_map/reduce_sum | solution.py:49
  418.0 4.7 subtract_convert_fusion
  422.7 19.4 %scatter_custom_fusion.1 = bf16[384,8192]{1,0:T(8,128)(2,1)} fusion(s32[256]{0:T(256)S(1)} %bitcast.70, bf16[128,8192]{1,0:T(8,128)(2,1)} %subtract_convert_fusion, s32[1024]{0:T(1024)S(1)} %pad_clamp_fusion.1, bf16[]{:T(256)} %constant.39.clone.1), kind=kCustom, calls=%fused_computation.15 | custom fusion | bytes 6291968 | tf_op jit(solution)/shard_map/scatter | solution.py:35
  442.2 10.9 %reshape.130 = bf16[64,3,2,8192]{3,2,1,0:T(2,128)(2,1)} reshape(bf16[384,8192]{1,0:T(8,128)(2,1)} %scatter_custom_fusion.1) | data formatting | bytes 12582912 | tf_op jit(solution)/shard_map/reshape | solution.py:36
  453.1 146.9 %all_to_all.15 = bf16[64,3,2,8192]{3,2,1,0:T(2,128)(2,1)S(1)} all-to-all(bf16[64,3,2,8192]{3,2,1,0:T(2,128)(2,1)} %reshape.130), channel_id=1, replica_groups=mesh['dp'=4,'latent'=64] {'latent'}, dimensions={0} | all-to-all | bytes 12582912 | tf_op jit(solution)/shard_map/all_to_all | solution.py:51
  600.0 7.2 fusion.50
  607.2 13.1 %fusion.5 = f32[3,64,8192,1]{2,1,3,0:T(8,128)} fusion(bf16[64,3,2,8192]{3,2,1,0:T(2,128)(2,1)} %all-to-all-done, bf16[64,3,2,64]{3,0,2,1:T(8,128)(2,1)S(1)} %get-tuple-element.4), kind=kOutput, calls=%fused_computation.11 | convolution fusion | flops 402653184 | bytes 12632064 | tf_op jit(solution)/shard_map/sbcd,sbce->dbe/dot_general | solution.py:56
  620.3 13.3 %fusion.1 = f32[3,64,8192,1]{2,1,3,0:T(8,128)} fusion(bf16[64,3,2,8192]{3,2,1,0:T(2,128)(2,1)} %copy-done.1, f32[64,3,2,64]{3,0,2,1:T(8,128)S(1)} %fusion.24), kind=kOutput, calls=%fused_computation.7 | convolution fusion | flops 404250624 | bytes 12681216 | tf_op jit(solution)/shard_map/sbce,sbcd->bed/dot_general | solution.py:60
  633.7 10.2 %psum.7 = f32[192]{0:T(256)} all-reduce(f32[192]{0:T(256)S(1)} %reshape.132), channel_id=1, replica_groups=mesh['dp'=4,'latent'=64] {'dp'}, use_global_device_ids=true, to_apply=%region_8.9 | all-reduce | flops 192 | bytes 1536 | tf_op jit(solution)/shard_map/psum | solution.py:64
  643.9 39.9 %reduce-scatter.3.cloned.1.call-done = f32[2048,192]{0,1:T(8,128)} async-done(((f32[8192,192]{0,1:T(8,128)}), f32[2048,192]{0,1:T(8,128)}) %reduce-scatter.3.cloned.1.call-update) | async-done | bytes 1572880 | tf_op jit(solution)/shard_map/reduce_scatter | solution.py:59
  683.9 69.3 %reduce-scatter.5.cloned.1.call-done = f32[192,2048]{1,0:T(8,128)} async-done(((f32[192,8192]{1,0:T(8,128)}), f32[192,2048]{1,0:T(8,128)}) %reduce-scatter.5.cloned.1.call-update) | async-done | bytes 1572880 | tf_op jit(solution)/shard_map/reduce_scatter | solution.py:63
  (24 shorter events, 0.6 us)
Async XLA Ops:
  7.2 200.3 %copy-start = (bf16[192,8192]{1,0:T(8,128)(2,1)S(1)}, bf16[192,8192]{1,0:T(8,128)(2,1)}, u32[]{:S(2)}) copy-start(bf16[192,8192]{1,0:T(8,128)(2,1)} %param.10) | copy-start | bytes 9437188
  42.1 13.7 %copy-start.3 = (f32[192]{0:T(256)S(1)}, f32[192]{0:T(256)}, u32[]{:S(2)}) copy-start(f32[192]{0:T(256)} %param.9) | copy-start | bytes 2308
  42.1 154.3 %all-to-all-start = ((bf16[64,3,2,8192]{3,2,1,0:T(2,128)(2,1)}), bf16[64,3,2,8192]{3,2,1,0:T(2,128)(2,1)}, u32[]{:S(2)}, u32[]{:S(2)}) async-start(bf16[64,3,2,8192]{3,2,1,0:T(2,128)(2,1)} %reshape.126), calls=%async_computation | async-start | bytes 12582912 | tf_op jit(solution)/shard_map/all_to_all | solution.py:38
  224.9 146.8 %all-to-all-start.1 = ((bf16[64,3,2,8192]{3,2,1,0:T(2,128)(2,1)}), bf16[64,3,2,8192]{3,2,1,0:T(2,128)(2,1)}, u32[]{:S(2)}, u32[]{:S(2)}) async-start(bf16[64,3,2,8192]{3,2,1,0:T(2,128)(2,1)} %copy.27), calls=%async_computation.1 | async-start | bytes 12582912 | tf_op jit(solution)/shard_map/all_to_all | solution.py:47
  230.8 453.0 %reduce-scatter.3.cloned.1.call-start = ((), (), s32[]{:S(2)}) async-start(), calls=%async_computation.5 | async-start | bytes 7864320 | tf_op jit(solution)/shard_map/reduce_scatter | solution.py:59
  404.5 13.5 %copy-start.2 = (f32[8192]{0:T(1024)S(1)}, f32[8192]{0:T(1024)}, u32[]{:S(2)}) copy-start(f32[8192]{0:T(1024)} %param.11) | copy-start | bytes 98308
  600.0 7.2 copy-start.1
  620.3 132.9 %reduce-scatter.5.cloned.1.call-start = ((), (), s32[]{:S(2)}) async-start(), calls=%async_computation.6 | async-start | bytes 7864320 | tf_op jit(solution)/shard_map/reduce_scatter | solution.py:63
Sparse Core Ops, SparseCore 0:
  620.4 63.3 reduce-scatter.2
  687.0 66.1 reduce-scatter.4
where the time goes:
time: 769 us; the launch traced here: 760 us
  waiting for transfers between devices  391 us (51%)
  blocking collectives  157 us (20%)
  local copies, waits for them, and re-layouts  112 us (15%)
  matrix products  46.6 us (6%)
  other arithmetic  20.1 us (3%)
  starting transfers between devices  19.7 us (3%)
  between operations  14.3 us (2%)
    all_to_all x1, blocking collectives, shards(): lax.all_to_all(dispatch(errors), 'latent', split_axis=0, concat_axis=0, t...  147 us
    all_to_all x1, waiting for transfers between devices, shards(): lax.all_to_all(part, 'latent', split_axis=0, concat_axis=0, tiled=True)  141 us
    all_to_all x1, waiting for transfers between devices, shards(): lax.all_to_all(dispatch(acts), 'latent', split_axis=0, concat_axis=0, til...  141 us
    reduce_scatter x1, waiting for transfers between devices, shards(): lax.psum_scatter(dec_term, 'dp', scatter_dimension=1, tiled=True)  69.3 us
    reduce_scatter x1, waiting for transfers between devices, shards(): lax.psum_scatter(enc_term, 'dp', scatter_dimension=0, tiled=True)  39.9 us
    scatter x2, local copies, waits for them, and re-layouts, dispatch(): jnp.zeros((padded_total, width), jnp.bfloat16).at[target]  38.9 us
    reshape x2, local copies, waits for them, and re-layouts, dispatch(): return filled.reshape(owners, local, room, width)  21.8 us
  transfers between devices with their start and end apart: 4, of which 4 were waited for; matrix products, arithmetic and copies ran while one was open for 2% of the time, Pallas kernels for 0%

commit v1 on v0

v1 whole, which is shorter than its diff:
```python
import functools

import jax
import jax.numpy as jnp
from jax import lax
from jax.experimental import pallas as pl
from jax.experimental.pallas import tpu as pltpu
from jax.sharding import PartitionSpec as P

F32, BF16 = jnp.float32, jnp.bfloat16
MESH = pl.DeviceIdType.MESH
ANY = pl.BlockSpec(memory_space=pl.ANY)
VMEM = pl.BlockSpec(memory_space=pltpu.VMEM)

NY, NX, NZ = 4, 4, 8
NP = NX * NZ
ROWS, D, BW, LOCAL = 128, 8192, 64, 192
DS = D // NP
SLOTS = NP * 6
LINES = NP * 3
BIG = 60 * 1024 * 1024
G_KIND = F32
PARTS = 2
PART = LINES // PARTS


def place():
    y, l = lax.axis_index("dp"), lax.axis_index("latent")
    return y, lax.div(l, 2), lax.rem(l, 2)


def shifted(p, step):
    x = lax.rem(lax.div(p, NZ) + lax.div(step, NZ), NX)
    z = lax.rem(lax.rem(p, NZ) + lax.rem(step, NZ), NZ)
    return x * NZ + z


def pair_of(p):
    return lax.div(p, 2 * NZ) * NZ + lax.rem(p, NZ)


def remote(src, dst, send, recv, device):
    return pltpu.make_async_remote_copy(
        src_ref=src, dst_ref=dst, send_sem=send, recv_sem=recv, device_id=device, device_id_type=MESH
    )


def wait_bytes(ref, sem):
    pltpu.make_async_copy(ref, ref, sem).wait()


def halves_of(v0, v1):
    return (jnp.concatenate([v0[:, 0:BW], v1[:, 0:BW]], axis=1),
            jnp.concatenate([v0[:, BW:128], v1[:, BW:128]], axis=1))


def by_chip(src, dst):
    def tile(t, _):
        v = [src[:, pl.ds(pl.multiple_of(q * (D // NY) + t * 128, 128), 128)].astype(F32) for q in range(NY)]
        even, odd = zip(halves_of(v[0], v[1]), halves_of(v[2], v[3]))
        for side, (e, o) in enumerate(((even[0], odd[0]), (even[1], odd[1]))):
            chip = lax.div(t, NZ) * 2 * NZ + lax.rem(t, NZ)
            dst[chip, :, pl.ds(side * 128, 128)] = e.astype(BF16)
            dst[chip + NZ, :, pl.ds(side * 128, 128)] = o.astype(BF16)
        return 0

    lax.fori_loop(0, NP // 2, tile, 0)


def spread_kernel(acts, info, w_enc, w_dec, acts_all, info_all, enc_all, dec_all,
                  own, own_acts, acts_cut, enc_cut, dec_cut, local_sem, send_sem, acts_sem, info_sem, enc_sem, dec_sem,
                  pair_sem, info_pair_sem, y_sem, far_sem, y_send):
    y, p, c = place()
    rows = pl.ds(pl.multiple_of(y * 48, 16), 48)
    loads = [pltpu.make_async_copy(w_enc.at[rows, :], own.at[0], local_sem.at[0]),
             pltpu.make_async_copy(w_dec.at[rows, :], own.at[1], local_sem.at[1]),
             pltpu.make_async_copy(acts, own_acts, local_sem.at[2])]
    for load in loads:
        load.start()
    barrier = pltpu.get_barrier_semaphore()

    def greet(i, _):
        pl.semaphore_signal(barrier, inc=1, device_id=(y, shifted(p, i) * 2 + c), device_id_type=MESH)
        return 0

    lax.fori_loop(1, NP, greet, 0)
    pl.semaphore_signal(barrier, inc=1, device_id=(y, p * 2 + 1 - c), device_id_type=MESH)
    for j in range(1, NY):
        pl.semaphore_signal(barrier, inc=1, device_id=(lax.rem(y + j, NY), p * 2 + c), device_id_type=MESH)
    loads[0].wait()
    by_chip(own.at[0], enc_cut)
    loads[1].wait()
    by_chip(own.at[1], dec_cut)
    pl.semaphore_wait(barrier, NP - 1 + 1 + NY - 1)

    mine = lax.div(p, NZ)
    pltpu.make_async_copy(enc_cut.at[p], enc_all.at[p, rows, :], enc_sem.at[mine]).start()
    pltpu.make_async_copy(dec_cut.at[p], dec_all.at[p, rows, :], dec_sem.at[mine]).start()
    pltpu.make_async_copy(info, info_all.at[c, p], info_sem.at[0]).start()

    def send_w(i, _):
        q = shifted(p, i)
        remote(enc_cut.at[q], enc_all.at[p, rows, :], send_sem.at[0], enc_sem.at[mine], (y, q * 2 + c)).start()
        remote(dec_cut.at[q], dec_all.at[p, rows, :], send_sem.at[1], dec_sem.at[mine], (y, q * 2 + c)).start()
        return 0

    lax.fori_loop(1, NP, send_w, 0)
    loads[2].wait()
    by_chip(own_acts, acts_cut)
    pltpu.make_async_copy(acts_cut.at[p], acts_all.at[c, p], acts_sem.at[mine]).start()

    def send_a(i, _):
        q = shifted(p, i)
        remote(info, info_all.at[c, p], send_sem.at[3], info_sem.at[0], (y, q * 2 + c)).start()
        remote(acts_cut.at[q], acts_all.at[c, p], send_sem.at[2], acts_sem.at[mine], (y, q * 2 + c)).start()
        return 0

    lax.fori_loop(1, NP, send_a, 0)

    up, down = lax.rem(y + 1, NY), lax.rem(y + NY - 1, NY)
    weights = ((enc_all, enc_sem, 0), (dec_all, dec_sem, 1))

    def pass_own(g):
        for ref, sem, n in weights:
            part = ref.at[pl.ds(g * NZ, NZ), rows, :]
            wait_bytes(part, sem.at[g])
            for side, v in enumerate((up, down)):
                remote(part, part, y_send.at[n], y_sem.at[n, side, g], (v, p * 2 + c)).start()

    def pass_on(g):
        for ref, _, n in weights:
            for side, (v, to) in enumerate(((down, up), (up, down))):
                theirs = pl.ds(pl.multiple_of(v * 48, 16), 48)
                wait_bytes(ref.at[pl.ds(g * NZ, NZ), theirs, :], y_sem.at[n, side, g])
                part = ref.at[pl.ds(g * NZ + side * (NZ // 2), NZ // 2), theirs, :]
                remote(part, part, y_send.at[n], far_sem.at[n, side], (to, p * 2 + c)).start()

    for i in range(NX + 1):
        if i < NX:
            pass_own(lax.rem(mine - i + NX, NX))
        if i > 0:
            pass_on(lax.rem(mine - i + 1 + NX, NX))
    pair = (y, p * 2 + 1 - c)
    wait_bytes(info_all.at[c], info_sem.at[0])
    remote(info_all.at[c], info_all.at[c], send_sem.at[4], info_pair_sem.at[0], pair).start()
    for i in range(NX):
        g = lax.rem(mine - i + NX, NX)
        part = acts_all.at[c, pl.ds(g * NZ, NZ)]
        wait_bytes(part, acts_sem.at[g])
        remote(part, part, send_sem.at[5], pair_sem.at[0], pair).start()

    wait_bytes(info_all.at[c], info_pair_sem.at[0])
    wait_bytes(acts_all.at[c], pair_sem.at[0])
    for n, ref in ((0, enc_all), (1, dec_all)):
        for side in range(2):
            wait_bytes(enc_cut.at[pl.ds(0, NP // 2)], far_sem.at[n, side])
        wait_bytes(ref.at[:, pl.ds(0, 144), :], y_send.at[n])
        wait_bytes(enc_cut.at[pl.ds(0, NP - 1)], send_sem.at[n])
    most = pl.ds(0, NP - 1)
    wait_bytes(acts_cut.at[most], send_sem.at[2])
    wait_bytes(info_all.at[0, most], send_sem.at[3])
    wait_bytes(info_all.at[0], send_sem.at[4])
    wait_bytes(acts_cut, send_sem.at[5])


def spread(acts, info, w_enc, w_dec):
    dma = pltpu.SemaphoreType.DMA
    return pl.pallas_call(
        spread_kernel,
        out_shape=(
            jax.ShapeDtypeStruct((2, NP, ROWS, DS), BF16),
            jax.ShapeDtypeStruct((2, NP, 16, 128), BF16),
            jax.ShapeDtypeStruct((NP, LOCAL, DS), BF16),
            jax.ShapeDtypeStruct((NP, LOCAL, DS), BF16),
        ),
        in_specs=[ANY] * 4,
        out_specs=(ANY,) * 4,
        scratch_shapes=[pltpu.VMEM((2, 48, D), BF16), pltpu.VMEM((ROWS, D), BF16),
                        pltpu.VMEM((NP, ROWS, DS), BF16), pltpu.VMEM((NP, 48, DS), BF16), pltpu.VMEM((NP, 48, DS), BF16),
                        dma((3,)), dma((6,)), dma((NX,)), dma((1,)), dma((NX,)), dma((NX,)), dma((1,)), dma((1,)),
                        dma((2, 2, NX)), dma((2, 2)), dma((2,))],
        compiler_params=pltpu.CompilerParams(collective_id=0, has_side_effects=True, vmem_limit_bytes=BIG),
        name="spread",
    )(acts, info, w_enc, w_dec)


def picks(info, c):
    half = c.astype(F32)
    slot = lax.broadcasted_iota(jnp.int32, (SLOTS, ROWS), 0).astype(F32)
    first = jnp.where(info[2:3] == half, info[0:1], -1.0)
    second = jnp.where(info[3:4] == half, info[1:2], -1.0)
    return ((slot == first) | (slot == second)).astype(F32).astype(BF16)


def low_half(shape):
    return lax.broadcasted_iota(jnp.int32, shape, 1) < BW


def lines_of(out):
    low = low_half((64, 128))
    a = jnp.where(low, out[0:64, 0:128], out[128:192, 0:128])
    b = jnp.where(low, out[64:128, 0:128], out[192:256, 0:128])
    d = jnp.concatenate([out[256:320, 128:192], out[320:384, 128:192]], axis=1)
    return a, b, d


def wide_of(a, b, d):
    low = low_half((64, 128))
    zero = jnp.zeros_like(a)
    top = jnp.concatenate(
        [jnp.where(low, a, zero), jnp.where(low, b, zero), jnp.where(low, zero, a), jnp.where(low, zero, b),
         zero, zero], axis=0)
    side = jnp.concatenate(
        [jnp.zeros((256, BW), a.dtype), d[:, 0:BW], d[:, BW:128]], axis=0)
    return jnp.concatenate([top, side], axis=1)


def store_by_slot(ref, s, value):
    ref[0, pl.ds(s, SLOTS, stride=64), :] = value[:, 0:128]
    ref[1, pl.ds(s, SLOTS, stride=64), :] = value[:, 128:256]


def load_owner(ref, o):
    rows = pl.ds(pl.multiple_of(o * 384, 384), 384)
    return jnp.concatenate([ref[0, rows, :], ref[1, rows, :]], axis=1)


def lines_out(lines, part, first, count):
    def body(s, _):
        part[s] = lines[pl.ds(s, LINES, stride=64), :].astype(part.dtype)
        return 0

    lax.fori_loop(first, first + count, body, 0, unroll=8)


def put_lines(lines, o, values):
    for k in range(3):
        lines[pl.ds(pl.multiple_of(o * 192 + k * 64, 64), 64), :] = values[k]


def get_lines(lines, o):
    return [lines[pl.ds(pl.multiple_of(o * 192 + k * 64, 64), 64), :] for k in range(3)]


def turn_in(source, lines):
    def body(s, _):
        lines[pl.ds(s, LINES, stride=64), :] = source[s].astype(F32)
        return 0

    lax.fori_loop(0, 64, body, 0, unroll=8)


CHUNKS = 4
S_STEP, O_STEP = 64 // CHUNKS, NP // CHUNKS
CHUNK_SEMS = pltpu.SemaphoreType.DMA((CHUNKS,))


def stream(src, dst, sems):
    k = src.shape[0] // CHUNKS
    return [pltpu.make_async_copy(src.at[pl.ds(i * k, k)], dst.at[pl.ds(i * k, k)], sems.at[i]) for i in range(CHUNKS)]


def start_all(*streams):
    for copies in streams:
        for copy in copies:
            copy.start()


def wait_all(*streams):
    for copies in streams:
        for copy in copies:
            copy.wait()


def encode_kernel(info_all, acts_hbm, enc_hbm, slots_hbm, part_hbm,
                  acts_all, enc_all, slots_out, part, slots, lines, a_sem, w_sem, s_sem, p_sem):
    _, _, c = place()
    acts_in, enc_in = stream(acts_hbm, acts_all, a_sem), stream(enc_hbm, enc_all, w_sem)
    out_slots, out_part = stream(slots_out, slots_hbm, s_sem), stream(part, part_hbm, p_sem)
    start_all(acts_in, enc_in)

    def expand(s, _):
        take = picks(info_all[s].astype(F32), c)
        store_by_slot(slots, s, jnp.dot(take, acts_all[s], preferred_element_type=F32))
        return 0

    def owner(o, _):
        inputs = load_owner(slots, o).astype(BF16)
        slots_out[o] = inputs
        put_lines(lines, o, lines_of(lax.dot_general(
            inputs, enc_all[o], (((1,), (1,)), ((), ())), preferred_element_type=F32)))
        return 0

    for i in range(CHUNKS):
        acts_in[i].wait()
        lax.fori_loop(i * S_STEP, (i + 1) * S_STEP, expand, 0, unroll=8)
    for i in range(CHUNKS):
        enc_in[i].wait()
        lax.fori_loop(i * O_STEP, (i + 1) * O_STEP, owner, 0, unroll=8)
        out_slots[i].start()
    for i in range(CHUNKS):
        lines_out(lines, part, i * S_STEP, S_STEP)
        out_part[i].start()
    wait_all(out_slots, out_part)


def encode(info_all, acts_all, enc_all):
    return pl.pallas_call(
        encode_kernel,
        out_shape=(
            jax.ShapeDtypeStruct((NP, 384, DS), BF16),
            jax.ShapeDtypeStruct((64, LINES, 128), F32),
        ),
        in_specs=[VMEM, ANY, ANY],
        out_specs=(ANY,) * 2,
        scratch_shapes=[pltpu.VMEM((64, ROWS, DS), BF16), pltpu.VMEM((NP, LOCAL, DS), BF16),
                        pltpu.VMEM((NP, 384, DS), BF16), pltpu.VMEM((64, LINES, 128), F32),
                        pltpu.VMEM((2, SLOTS * 64, 128), F32), pltpu.VMEM((LINES * 64, 128), F32)] + [CHUNK_SEMS] * 4,
        compiler_params=pltpu.CompilerParams(vmem_limit_bytes=BIG),
        name="encode",
    )(info_all, acts_all, enc_all)


def decode_kernel(info_all, codes, dec_hbm, recon_hbm, other_hbm, wide_hbm,
                  dec_all, recon, wide_out, slots, lines, w_sem, r_sem, o_sem, send_sem, recv_sem):
    y, p, c = place()
    pair = (y, p * 2 + 1 - c)
    barrier = pltpu.get_barrier_semaphore()
    pl.semaphore_signal(barrier, inc=1, device_id=pair, device_id_type=MESH)
    dec_in = stream(dec_hbm, dec_all, w_sem)
    out_recon, out_wide = stream(recon, recon_hbm, r_sem), stream(wide_out, wide_hbm, o_sem)
    start_all(dec_in)
    turn_in(codes, lines)

    def owner(o, _):
        wide = wide_of(*get_lines(lines, o)).astype(BF16)
        wide_out[o] = wide
        part = jnp.dot(wide, dec_all[o], preferred_element_type=F32)
        rows = pl.ds(pl.multiple_of(o * 384, 384), 384)
        slots[0, rows, :] = part[:, 0:128]
        slots[1, rows, :] = part[:, 128:256]
        return 0

    def gather(s, _):
        take = picks(info_all[s].astype(F32), c)
        part = jnp.concatenate(
            [slots[h, pl.ds(s, SLOTS, stride=64), :].astype(BF16) for h in range(2)], axis=1)
        recon[s] = lax.dot_general(
            take, part, (((0,), (0,)), ((), ())), preferred_element_type=F32).astype(BF16)
        return 0

    for i in range(CHUNKS):
        dec_in[i].wait()
        lax.fori_loop(i * O_STEP, (i + 1) * O_STEP, owner, 0, unroll=8)
        out_wide[i].start()
    pl.semaphore_wait(barrier, 1)
    sent = []
    for i in range(CHUNKS):
        lax.fori_loop(i * S_STEP, (i + 1) * S_STEP, gather, 0, unroll=8)
        out_recon[i].start()
        rows = pl.ds(i * S_STEP, S_STEP)
        sent.append(remote(recon.at[rows], other_hbm.at[rows], send_sem.at[i], recv_sem.at[i], pair))
        sent[i].start()
    wait_all(out_recon, out_wide, sent)


def decode(info_all, codes, dec_all):
    return pl.pallas_call(
        decode_kernel,
        out_shape=(
            jax.ShapeDtypeStruct((64, ROWS, DS), BF16),
            jax.ShapeDtypeStruct((64, ROWS, DS), BF16),
            jax.ShapeDtypeStruct((NP, 384, LOCAL), BF16),
        ),
        in_specs=[VMEM, VMEM, ANY],
        out_specs=(ANY,) * 3,
        scratch_shapes=[pltpu.VMEM((NP, LOCAL, DS), BF16), pltpu.VMEM((64, ROWS, DS), BF16),
                        pltpu.VMEM((NP, 384, LOCAL), BF16),
                        pltpu.VMEM((2, SLOTS * 64, 128), F32), pltpu.VMEM((LINES * 64, 128), F32)] + [CHUNK_SEMS] * 5,
        compiler_params=pltpu.CompilerParams(collective_id=4, has_side_effects=True, vmem_limit_bytes=BIG),
        name="decode",
    )(info_all, codes, dec_all)


def pack_owners(out, i, v0, v1):
    h, u = lax.div(i, 8), lax.rem(i, 8)
    for side in range(2):
        tile = slice(side * 128, side * 128 + 128)
        low, high = halves_of(v0[:, tile], v1[:, tile])
        out[2 * side, h, u] = low.astype(BF16)
        out[2 * side + 1, h, u] = high.astype(BF16)


OVER_ROWS = (((0,), (0,)), ((), ()))


def errors_kernel(info_all, b_dec, acts_hbm, mine_hbm, other_hbm, dec_hbm, wide_hbm, part, dec,
                  acts_all, mine, other, dec_all, wide, slots, lines, *sems):
    _, _, c = place()
    ins = [stream(src, dst, sem) for src, dst, sem in zip(
        (acts_hbm, mine_hbm, other_hbm, dec_hbm, wide_hbm), (acts_all, mine, other, dec_all, wide), sems)]
    for i in range(CHUNKS):
        start_all([copies[i] for copies in ins[0:3]])
    start_all(*ins[3:])

    def expand(s, _):
        recon = mine[s].astype(F32) + other[s].astype(F32)
        errors = (recon + b_dec[0:1] - acts_all[s].astype(F32)).astype(BF16)
        take = picks(info_all[s].astype(F32), c)
        store_by_slot(slots, s, jnp.dot(take, errors, preferred_element_type=F32))
        return 0

    def product(o):
        wanted = load_owner(slots, o).astype(BF16)
        grad = lax.dot_general(wanted, dec_all[o], (((1,), (1,)), ((), ())), preferred_element_type=F32)
        put_lines(lines, o, lines_of(grad))
        return lax.dot_general(wide[o], wanted, OVER_ROWS, preferred_element_type=F32)

    def owners(i, _):
        pack_owners(dec, i, product(2 * i), product(2 * i + 1))
        return 0

    for i in range(CHUNKS):
        wait_all([copies[i] for copies in ins[0:3]])
        lax.fori_loop(i * S_STEP, (i + 1) * S_STEP, expand, 0, unroll=8)
    for i in range(CHUNKS):
        wait_all([copies[i] for copies in ins[3:]])
        lax.fori_loop(i * O_STEP // 2, (i + 1) * O_STEP // 2, owners, 0, unroll=4)
    lines_out(lines, part, 0, 64)


def errors_of(info_all, acts_all, mine, other, b_dec, dec_all, wide, kind):
    return pl.pallas_call(
        errors_kernel,
        out_shape=(
            jax.ShapeDtypeStruct((64, LINES, 128), kind),
            jax.ShapeDtypeStruct((NY, 2, 8, LOCAL, 128), BF16),
        ),
        in_specs=[VMEM] * 2 + [ANY] * 5,
        out_specs=(VMEM,) * 2,
        scratch_shapes=[pltpu.VMEM((64, ROWS, DS), BF16)] * 3
        + [pltpu.VMEM((NP, LOCAL, DS), BF16), pltpu.VMEM((NP, 384, LOCAL), BF16),
           pltpu.VMEM((2, SLOTS * 64, 128), F32), pltpu.VMEM((LINES * 64, 128), F32)] + [CHUNK_SEMS] * 5,
        compiler_params=pltpu.CompilerParams(vmem_limit_bytes=BIG),
        name="errors",
    )(info_all, b_dec, acts_all, mine, other, dec_all, wide)


def enc_grads_kernel(g_all, inputs_hbm, enc, bias, inputs, lines, i_sem):
    inputs_in = stream(inputs_hbm, inputs, i_sem)
    start_all(inputs_in)
    turn_in(g_all, lines)

    def product(o):
        a, b, d = get_lines(lines, o)
        bias[o] = jnp.concatenate(
            [jnp.sum(a + b, axis=0, keepdims=True), jnp.sum(d, axis=0, keepdims=True), jnp.zeros((6, 128), F32)], axis=0)
        return lax.dot_general(wide_of(a, b, d).astype(BF16), inputs[o], OVER_ROWS, preferred_element_type=F32)

    def owners(i, _):
        pack_owners(enc, i, product(2 * i), product(2 * i + 1))
        return 0

    for i in range(CHUNKS):
        inputs_in[i].wait()
        lax.fori_loop(i * O_STEP // 2, (i + 1) * O_STEP // 2, owners, 0, unroll=4)


def enc_grads(g_all, inputs):
    return pl.pallas_call(
        enc_grads_kernel,
        out_shape=(
            jax.ShapeDtypeStruct((NY, 2, 8, LOCAL, 128), BF16),
            jax.ShapeDtypeStruct((NP, 8, 128), F32),
        ),
        in_specs=[VMEM, ANY],
        out_specs=(VMEM,) * 2,
        scratch_shapes=[pltpu.VMEM((NP, 384, DS), BF16), pltpu.VMEM((LINES * 64, 128), F32), CHUNK_SEMS],
        compiler_params=pltpu.CompilerParams(vmem_limit_bytes=BIG),
        name="enc_grads",
    )(g_all, inputs)


def meet_peers(y, p, c):
    side = lax.rem(lax.div(p, NZ), 2)

    def at(v, h):
        return (v, (p + (h - side) * NZ) * 2 + c)

    return side, lax.rem(y + 1, NY), lax.rem(y + NY - 1, NY), lax.rem(y + 2, NY), at


def meet_greet(y, p, c, barrier):
    side, up, down, far, at = meet_peers(y, p, c)
    for v in (up, down, far):
        for h in range(2):
            pl.semaphore_signal(barrier, inc=1, device_id=at(v, h), device_id_type=MESH)


MEET_PARTS = 2
MEET_ROWS = LOCAL // MEET_PARTS


def meet_rows(n):
    return pl.ds(n * MEET_ROWS, MEET_ROWS)


def meet_start(y, p, c, src, land, relay, send, recv):
    side, up, down, far, at = meet_peers(y, p, c)
    low, high = pl.ds(0, 4), pl.ds(4, 4)
    for n in range(MEET_PARTS):
        rows = meet_rows(n)
        remote(src.at[far, :, low, rows], relay.at[0, :, :, rows], send.at[0], recv.at[n, 0], at(up, side)).start()
        remote(src.at[far, :, high, rows], relay.at[1, :, :, rows], send.at[0], recv.at[n, 1], at(down, side)).start()
        for h in range(2):
            remote(src.at[up, h, high, rows], land.at[side, 1, high, rows], send.at[1], recv.at[n, 2], at(up, h)).start()
            remote(src.at[down, h, low, rows], land.at[side, 2, low, rows], send.at[1], recv.at[n, 2],
                   at(down, h)).start()
        pltpu.make_async_copy(src.at[y, side, :, rows], land.at[side, 0, :, rows], recv.at[n, 2]).start()
        remote(src.at[y, 1 - side, :, rows], land.at[side, 0, :, rows], send.at[1], recv.at[n, 2],
               at(y, 1 - side)).start()


def meet_merge(y, p, c, n, src, land, relay, merged, send, recv):
    side, up, down, far, at = meet_peers(y, p, c)
    rows = meet_rows(n)
    for k, (v, first) in enumerate(((up, 0), (down, 4))):
        wait_bytes(relay.at[k, :, :, rows], recv.at[n, k])
        for h in range(2):

            def add(i, _):
                merged[k, h, i, rows] = (
                    src[v, h, first + i, rows].astype(F32) + relay[k, h, i, rows].astype(F32)).astype(BF16)
                return 0

            lax.fori_loop(0, 4, add, 0)
            remote(merged.at[k, h, :, rows], land.at[side, 1 + k, pl.ds(first, 4), rows], send.at[1], recv.at[n, 2],
                   at(v, h)).start()


def meet_wait(n, land, recv):
    wait_bytes(land.at[:, :, :, meet_rows(n)], recv.at[n, 2])


def meet_sum(land, total, u, n):
    def tile(t, _):
        rows = pl.ds(pl.multiple_of(n * MEET_ROWS + t * 32, 32), 32)
        v = [land[e, 0, u, rows, :].astype(F32) + land[e, 1, u, rows, :].astype(F32) + land[e, 2, u, rows, :].astype(F32)
             for e in range(2)]
        low, high = halves_of(v[0], v[1])
        total[2 * u, rows, :], total[2 * u + 1, rows, :] = low.astype(BF16), high.astype(BF16)
        return 0

    lax.fori_loop(0, MEET_ROWS // 32, tile, 0)


def meet_end(land, relay, send):
    wait_bytes(relay, send.at[0])
    wait_bytes(land.at[0], send.at[1])
    wait_bytes(land.at[0, 0], send.at[1])
    wait_bytes(land.at[0, 0], send.at[1])


MEET_SCRATCH = [pltpu.VMEM((2, 3, 8, LOCAL, 128), BF16), pltpu.VMEM((2, 2, 4, LOCAL, 128), BF16),
                pltpu.VMEM((2, 2, 4, LOCAL, 128), BF16), pltpu.SemaphoreType.DMA((2,)), pltpu.SemaphoreType.DMA((MEET_PARTS, 3))]


def slope_of(v):
    return 0.5 * (1.0 + lax.erf(v * 0.7071067811865476)) + v * jnp.exp(-0.5 * v * v) * 0.3989422804014327


def exchange_kernel(forward, part, extra, *rest):
    if forward:
        (out_all, slope_out, got, code, x_relay, x_merged, x_land, z_out, send_sem, xr_sem, xl_sem, recv_sem,
         line_sem, x_sem, far_sem, back_sem) = rest
    else:
        (dec, out_all, dec_total, got, code, x_relay, x_merged, x_land, z_out, send_sem, xr_sem, xl_sem, recv_sem,
         line_sem, x_sem, far_sem, back_sem, land, relay, merged, m_send, m_recv) = rest
    y, p, c = place()
    x, z = lax.div(p, NZ), lax.rem(p, NZ)
    barrier = pltpu.get_barrier_semaphore()

    right, left = lax.rem(x + 1, NX), lax.rem(x + NX - 1, NX)
    far = lax.rem(x + 2, NX)

    def in_line(i):
        return lax.rem(z + lax.rem(i, NZ), NZ), lax.rem(c + lax.div(i, NZ), 2)

    def greet(i, _):
        w, h = in_line(i)
        pl.semaphore_signal(barrier, inc=1, device_id=(y, (x * NZ + w) * 2 + h), device_id_type=MESH)
        return 0

    lax.fori_loop(1, 2 * NZ, greet, 0)
    for v in (right, left):
        pl.semaphore_signal(barrier, inc=1, device_id=(y, (v * NZ + z) * 2 + c), device_id_type=MESH)
    if not forward:
        meet_greet(y, p, c, barrier)
    pl.semaphore_wait(barrier, 17 if forward else 23)

    def beside(v):
        return (y, (v * NZ + z) * 2 + c)

    def cut(ref, n):
        return ref.at[..., pl.ds(n * PART, PART), :]

    def rows_of(v, k, n):
        return part.at[k, pl.ds(v * NZ, NZ), pl.ds(n * PART, PART)]

    ways = ((right, left, 0), (left, right, 1))
    for n in range(PARTS):
        for to, _, k in ways:
            remote(rows_of(far, k, n), cut(x_relay.at[k], n), send_sem.at[0], xr_sem.at[n, k], beside(to)).start()
        for to, _, k in ways:
            remote(rows_of(to, 1 - k, n), cut(x_land.at[k, 1 - k], n), send_sem.at[1], xl_sem.at[n], beside(to)).start()
    for n in range(PARTS):
        own = pl.ds(n * PART, PART)
        for to, _, k in ways:
            wait_bytes(cut(x_relay.at[k], n), xr_sem.at[n, k])

            def merge(w, _):
                x_merged[k, w, own] = (
                    part[k, to * NZ + w, own].astype(F32) + x_relay[k, w, own].astype(F32)).astype(part.dtype)
                return 0

            lax.fori_loop(0, NZ, merge, 0)
            remote(cut(x_merged.at[k], n), cut(x_land.at[k, k], n), send_sem.at[1], xl_sem.at[n], beside(to)).start()
    for n in range(PARTS):
        own = pl.ds(n * PART, PART)
        wait_bytes(cut(x_land, n), xl_sem.at[n])

        def z_send(i, _):
            w, h = in_line(i)
            z_out[h, w, own] = (part[h, x * NZ + w, own].astype(F32) + x_land[0, h, w, own].astype(F32)
                                + x_land[1, h, w, own].astype(F32))
            source, target = z_out.at[h, w, own], got.at[c, z, own]

            @pl.when(i > 0)
            def _():
                remote(source, target, send_sem.at[2], recv_sem.at[n], (y, (x * NZ + w) * 2 + h)).start()

            @pl.when(i == 0)
            def _():
                pltpu.make_async_copy(source, target, recv_sem.at[n]).start()

            return 0

        lax.fori_loop(0, 2 * NZ, z_send, 0)

    if not forward:
        meet_start(y, p, c, dec, land, relay, m_send, m_recv)

    for n in range(PARTS):
        own = pl.ds(n * PART, PART)
        wait_bytes(cut(got, n), recv_sem.at[n])
        for h in range(2):
            for t in range(PART // 16):
                rows = pl.ds(n * PART + t * 16, 16)
                total = got[h, 0, rows, :]
                for q in range(1, NZ):
                    total = total + got[h, q, rows, :]
                if forward:
                    pre = total + extra[h, rows, :]
                    slope_out[h, rows, :] = slope_of(pre)
                    code[h, rows, :] = (pre * 0.5 * (1.0 + lax.erf(pre * 0.7071067811865476))).astype(BF16)
                else:
                    code[h, rows, :] = (total * extra[h, rows, :]).astype(BF16)
        pltpu.make_async_copy(code.at[c, own], out_all.at[c, p, own], line_sem.at[n]).start()

        def share(i, _):
            w, h = in_line(i)
            remote(code.at[h, own], out_all.at[c, p, own], back_sem.at[0], line_sem.at[n],
                   (y, (x * NZ + w) * 2 + h)).start()
            return 0

        lax.fori_loop(1, 2 * NZ, share, 0)

    if not forward:
        for n in range(MEET_PARTS):
            meet_merge(y, p, c, n, dec, land, relay, merged, m_send, m_recv)

    def line(v, k, n):
        return out_all.at[k, pl.ds(v * NZ, NZ), pl.ds(n * PART, PART)]

    for n in range(PARTS):
        wait_bytes(cut(out_all.at[:, pl.ds(0, NZ)], n), line_sem.at[n])
        for side, v in enumerate((right, left)):
            for k in (side, 1 - side):
                remote(line(x, k, n), line(x, k, n), back_sem.at[1], x_sem.at[n, side, k], beside(v)).start()
    for n in range(PARTS):
        for side, (v, to) in enumerate(((left, right), (right, left))):
            wait_bytes(line(v, side, n), x_sem.at[n, side, side])
            remote(line(v, side, n), line(v, side, n), back_sem.at[2], far_sem.at[n, side], beside(to)).start()
    if not forward:
        for n in range(MEET_PARTS):
            meet_wait(n, land, m_recv)

            def total_of(u, _):
                meet_sum(land, dec_total, u, n)
                return 0

            lax.fori_loop(0, 8, total_of, 0)
    for n in range(PARTS):
        for side, v in enumerate((left, right)):
            wait_bytes(line(v, 1 - side, n), x_sem.at[n, side, 1 - side])
            wait_bytes(line(v, 0, n), far_sem.at[n, side])
    wait_bytes(x_relay, send_sem.at[0])
    wait_bytes(x_land, send_sem.at[1])
    wait_bytes(got.at[0], send_sem.at[2])
    wait_bytes(got.at[0, pl.ds(0, NZ - 1)], send_sem.at[2])
    wait_bytes(out_all.at[0, pl.ds(0, 2 * NZ - 1)], back_sem.at[0])
    wait_bytes(out_all.at[0], back_sem.at[1])
    wait_bytes(out_all.at[0, pl.ds(0, 2 * NZ)], back_sem.at[2])
    if not forward:
        meet_end(land, relay, m_send)


def exchange(forward, part, extra, *dec):
    dma = pltpu.SemaphoreType.DMA
    out = [jax.ShapeDtypeStruct((2, NP, LINES, 128), BF16)]
    if forward:
        out.append(jax.ShapeDtypeStruct((2, LINES, 128), F32))
    else:
        out.append(jax.ShapeDtypeStruct((16, LOCAL, 128), BF16))
    return pl.pallas_call(
        functools.partial(exchange_kernel, forward),
        out_shape=tuple(out),
        in_specs=[VMEM] * (2 + len(dec)),
        out_specs=(VMEM,) * len(out),
        scratch_shapes=[pltpu.VMEM((2, NZ, LINES, 128), F32), pltpu.VMEM((2, LINES, 128), BF16),
                        pltpu.VMEM((2, NZ, LINES, 128), part.dtype), pltpu.VMEM((2, NZ, LINES, 128), part.dtype),
                        pltpu.VMEM((2, 2, NZ, LINES, 128), part.dtype), pltpu.VMEM((2, NZ, LINES, 128), F32),
                        dma((3,)), dma((PARTS, 2)), dma((PARTS,)), dma((PARTS,)), dma((PARTS,)), dma((PARTS, 2, 2)),
                        dma((PARTS, 2)), dma((3,))]
        + ([] if forward else MEET_SCRATCH),
        compiler_params=pltpu.CompilerParams(
            collective_id=1 if forward else 2, has_side_effects=True, vmem_limit_bytes=BIG),
        name="exchange_code" if forward else "exchange_grad",
    )(part.reshape(2, NP, LINES, 128), extra, *dec)


def deliver_kernel(enc, dec_total, bias, enc_out, dec_out, bias_out, bias_y, enc_total, b_send, b_recv,
                   send_sem, recv_sem, land, relay, merged, m_send, m_recv):
    y, p, c = place()
    x, z = lax.div(p, NZ), lax.rem(p, NZ)
    side = lax.rem(x, 2)
    barrier = pltpu.get_barrier_semaphore()

    def greet(i, _):
        pl.semaphore_signal(barrier, inc=1, device_id=(y, shifted(p, i) * 2 + c), device_id_type=MESH)
        return 0

    lax.fori_loop(1, NP, greet, 0)
    meet_greet(y, p, c, barrier)
    pl.semaphore_wait(barrier, NP - 1 + 6)

    here = pair_of(p)

    def to_owners(total, out, n, u, rows):
        for e in range(2):
            o = side * 2 * NZ + 2 * u + e

            @pl.when(o != p)
            def _():
                remote(total.at[2 * u + e, rows], out.at[here, rows], send_sem.at[n], recv_sem.at[n], (y, o * 2 + c)).start()

            @pl.when(o == p)
            def _():
                pltpu.make_async_copy(total.at[2 * u + e, rows], out.at[here, rows], recv_sem.at[n]).start()

    def turned(i):
        return lax.rem(i + lax.div(z, 2), 8)

    meet_start(y, p, c, enc, land, relay, m_send, m_recv)
    pltpu.make_async_copy(bias.at[p], bias_y.at[y], b_recv.at[0]).start()
    for j in range(1, NY):
        remote(bias.at[p], bias_y.at[y], b_send.at[0], b_recv.at[0], (lax.rem(y + j, NY), p * 2 + c)).start()

    def dec_owner(i, _):
        to_owners(dec_total, dec_out, 0, turned(i), pl.ds(0, LOCAL))
        return 0

    lax.fori_loop(0, 8, dec_owner, 0)
    for n in range(MEET_PARTS):
        meet_merge(y, p, c, n, enc, land, relay, merged, m_send, m_recv)
    for n in range(MEET_PARTS):
        meet_wait(n, land, m_recv)

        def enc_owner(i, _):
            u = turned(i)
            meet_sum(land, enc_total, u, n)
            to_owners(enc_total, enc_out, 1, u, meet_rows(n))
            return 0

        lax.fori_loop(0, 8, enc_owner, 0)
    wait_bytes(bias_y, b_recv.at[0])
    bias_out[...] = bias_y[0] + bias_y[1] + bias_y[2] + bias_y[3]
    wait_bytes(bias_y.at[pl.ds(0, NY - 1)], b_send.at[0])
    meet_end(land, relay, m_send)
    for n in range(2):
        wait_bytes(enc_total, recv_sem.at[n])
        wait_bytes(enc_total.at[pl.ds(0, 15)], send_sem.at[n])

        @pl.when(lax.div(x, 2) != side)
        def _():
            wait_bytes(enc_total.at[0], send_sem.at[n])


def deliver(enc, dec_total, bias):
    dma = pltpu.SemaphoreType.DMA
    return pl.pallas_call(
        deliver_kernel,
        out_shape=(
            jax.ShapeDtypeStruct((16, LOCAL, 128), BF16),
            jax.ShapeDtypeStruct((16, LOCAL, 128), BF16),
            jax.ShapeDtypeStruct((8, 128), F32),
        ),
        in_specs=[VMEM, VMEM, ANY],
        out_specs=(ANY, ANY, VMEM),
        scratch_shapes=[pltpu.VMEM((NY, 8, 128), F32), pltpu.VMEM((16, LOCAL, 128), BF16),
                        dma((1,)), dma((1,)), dma((2,)), dma((2,))] + MEET_SCRATCH,
        compiler_params=pltpu.CompilerParams(collective_id=3, has_side_effects=True, vmem_limit_bytes=BIG),
        name="deliver",
    )(enc, dec_total, bias)


def info_kernel(blocks, b_enc, out):
    numbers = blocks[...]
    first, second = numbers[0:1].astype(F32), numbers[1:2].astype(F32)
    square = (ROWS, ROWS)
    before = lax.broadcasted_iota(jnp.int32, square, 0) < lax.broadcasted_iota(jnp.int32, square, 1)
    first_down = jnp.transpose(jnp.broadcast_to(first, square))
    second_down = jnp.transpose(jnp.broadcast_to(second, square))

    def count(hit):
        return jnp.sum(jnp.where(hit, 1, 0), axis=0, keepdims=True)

    rank = jnp.concatenate([
        count((first_down == first) & before),
        count(first_down == second) + count((second_down == second) & before)], axis=0)
    owner = lax.div(numbers, 3)
    slot = (lax.div(owner, 2) * 3 + lax.rem(numbers, 3)) * 2 + rank
    bias = b_enc[...]
    line = jnp.concatenate(
        [bias[:, 0:128], bias[:, 0:128], jnp.concatenate([bias[:, 128:192], bias[:, 128:192]], axis=1)], axis=0)
    top = line.astype(BF16).astype(F32)
    middle = (line - top).astype(BF16).astype(F32)
    out[...] = jnp.concatenate(
        [slot.astype(F32), lax.rem(owner, 2).astype(F32), top, middle, line - top - middle, jnp.zeros((3, ROWS), F32)],
        axis=0).astype(BF16)


def info_of(blocks, b_enc):
    return pl.pallas_call(
        info_kernel,
        out_shape=jax.ShapeDtypeStruct((16, ROWS), BF16),
        in_specs=[VMEM] * 2,
        out_specs=VMEM,
        name="info",
    )(blocks.T, b_enc.reshape(1, LOCAL))


def shards(acts, blocks, w_enc, b_enc, w_dec, b_dec):
    l = lax.axis_index("latent")
    p = l // 2
    acts_all, info_all, enc_all, dec_all = spread(acts, info_of(blocks, b_enc), w_enc.T, w_dec)
    acts_all = acts_all.reshape(64, ROWS, DS)
    info_all = info_all.reshape(64, 16, 128)
    inputs, part = encode(info_all, acts_all, enc_all)
    bias = info_all.astype(F32)
    bias = (bias[:, 4:7] + bias[:, 7:10] + bias[:, 10:13]).reshape(2, LINES, 128)
    codes, slope = exchange(True, part, bias)
    recon, other, wide = decode(info_all, codes.reshape(64, LINES, 128), dec_all)
    my_b_dec = lax.dynamic_slice(b_dec.reshape(NY, D // NY), (0, pair_of(p) * 128 + p // NZ % 2 * 64), (NY, 64))
    my_b_dec = jnp.broadcast_to(my_b_dec.reshape(1, DS), (8, DS))
    g_part, dec = errors_of(info_all, acts_all, recon, other, my_b_dec, dec_all, wide, G_KIND)
    g_all, dec_total = exchange(False, g_part, slope, dec)
    enc, bias_sum = enc_grads(g_all.reshape(64, LINES, 128), inputs)
    enc_tiles, dec_tiles, lines = deliver(enc, dec_total, bias_sum)
    grad_b_enc = jnp.concatenate([lines[0], lines[1, 0:64] + lines[1, 64:128]])

    def whole(tiles):
        return tiles.transpose(1, 0, 2).reshape(LOCAL, D // NY).astype(F32)

    return whole(enc_tiles).T, grad_b_enc, whole(dec_tiles)


def solution(mesh):
    return jax.shard_map(
        shards,
        mesh=mesh,
        in_specs=(
            P(("dp", "latent"), None),
            P(("dp", "latent"), None),
            P(None, "latent"),
            P("latent"),
            P("latent", None),
            P(),
        ),
        out_specs=(P("dp", "latent"), P("latent"), P("latent", "dp")),
        check_vma=False,
    )
```

time: 769 us -> 390 us (0.51); the launches traced: 760 us -> 390 us
  waiting for transfers between devices: 391 us -> 0 us
  Pallas kernels: 0 us -> 379 us
  blocking collectives: 157 us -> 0 us
  local copies, waits for them, and re-layouts: 112 us -> 5.56 us
  matrix products: 46.6 us -> 0 us
  starting transfers between devices: 19.7 us -> 0 us
  other arithmetic: 20.1 us -> 4.19 us
  between operations: 14.3 us -> 0.78 us
    pallas_call x0 -> x9, Pallas kernels: none -> 379 us  [the longest x2 142 us: exchange(): pl.pallas_call(functools.partial(exchange_kernel, forward), out_shape=tup...]
    all_to_all x2 -> x0, waiting for transfers between devices: 281 us -> none  [the longest x1 141 us: shards(): lax.all_to_all(part, 'latent', split_axis=0, concat_axis=0, tiled=True)]
    all_to_all x1 -> x0, blocking collectives: 147 us -> none  [shards(): lax.all_to_all(dispatch(errors), 'latent', split_axis=0, concat_axis=0, t...]
    reduce_scatter x2 -> x0, waiting for transfers between devices: 109 us -> none  [the longest x1 69.3 us: shards(): lax.psum_scatter(dec_term, 'dp', scatter_dimension=1, tiled=True)]
    dot_general x5 -> x0, matrix products: 46.6 us -> none  [the longest x1 13.3 us: shards(): jnp.einsum('sbce,sbcd->bed', code, wanted, preferred_element_type=jnp.flo...]
    scatter x2 -> x0, local copies, waits for them, and re-layouts: 38.9 us -> none  [dispatch(): jnp.zeros((padded_total, width), jnp.bfloat16).at[target]]
    reshape x4 -> x2, local copies, waits for them, and re-layouts: 32.4 us -> 1.46 us  [the longest x1 0.77 us: shards(): b_dec.reshape(NY, D // NY)]
    convert_element_type x2 -> x1, local copies, waits for them, and re-layouts: 25 us -> 1.32 us  [whole(): return tiles.transpose(1, 0, 2).reshape(LOCAL, D // NY).astype(F32)]
  transfers between devices with their start and end apart: 4 -> 0, of which waited for: 4 -> 0; matrix products, arithmetic and copies ran while one was open for 2% -> 0% of each run, Pallas kernels for 0% -> 0%
where the time goes in v1:
time: 390 us
  Pallas kernels  379 us (97%)
  local copies, waits for them, and re-layouts  5.56 us (1%)
  other arithmetic  4.19 us (1%)
    pallas_call x2, Pallas kernels, exchange(): pl.pallas_call(functools.partial(exchange_kernel, forward), out_shape=tup...  142 us
    pallas_call x1, Pallas kernels, spread(): pl.pallas_call(spread_kernel, out_shape=(jax.ShapeDtypeStruct((2, NP, ROW...  99 us
    pallas_call x1, Pallas kernels, deliver(): pl.pallas_call(deliver_kernel, out_shape=(jax.ShapeDtypeStruct((16, LOCAL...  61.6 us
    pallas_call x1, Pallas kernels, errors_of(): pl.pallas_call(errors_kernel, out_shape=(jax.ShapeDtypeStruct((64, LINES,...  25 us
    pallas_call x1, Pallas kernels, decode(): pl.pallas_call(decode_kernel, out_shape=(jax.ShapeDtypeStruct((64, ROWS,...  20.4 us
    pallas_call x1, Pallas kernels, encode(): pl.pallas_call(encode_kernel, out_shape=(jax.ShapeDtypeStruct((NP, 384, D...  19.1 us
    pallas_call x1, Pallas kernels, enc_grads(): pl.pallas_call(enc_grads_kernel, out_shape=(jax.ShapeDtypeStruct((NY, 2,...  10.1 us

profile of v1, /device:TPU:1, one launch (start us, length us, event | category | flops | bytes accessed | tf_op | source)
XLA Modules:
  0.0 389.6 jit_solution(11510153303069104662)
XLA Ops:
  0.7 1.4 info.1
  2.1 0.8 reshape.44
  2.9 0.1 constant_dynamic-slice_fusion
  3.0 0.1 broadcast_in_dim.7
  3.0 0.6 broadcast_in_dim.8.b_dec
  3.7 99.0 %spread.1 = (bf16[2,32,128,256]{3,2,1,0:T(8,128)(2,1)}, bf16[2,32,16,128]{3,2,1,0:T(8,128)(2,1)}, bf16[32,192,256]{2,1,0:T(8,128)(2,1)}, bf16[32,192,256]{2,1,0:T(8,128)(2,1)}) custom-call(bf16[128,8192]{1,0:T(8,128)(2,1)} %acts.1, bf16[16,128]{1,0:T(8,128)(2,1)} %info.1, bf16[192,8192]{1,0:T(8,128)(2,1)} %bitcast.36, bf16[192,8192]{1,0:T(8,128)(2,1)} %w_dec.1), custom_call_target="tpu_custom_call" | custom-call | tf_op jit(solution)/shard_map/spread/pallas_call | solution.py:168
  102.7 1.0 bitcast_convert_fusion
  103.7 0.1 slice_add_fusion
  103.8 0.7 reshape.47.extra
  104.5 19.1 %encode.1 = (bf16[32,384,256]{2,1,0:T(8,128)(2,1)}, f32[64,96,128]{2,1,0:T(8,128)}) custom-call(bf16[64,16,128]{2,1,0:T(8,128)(2,1)} %bitcast.31, bf16[64,128,256]{2,1,0:T(8,128)(2,1)} %bitcast.29, bf16[32,192,256]{2,1,0:T(8,128)(2,1)} %get-tuple-element.25.enc_hbm), custom_call_target="tpu_custom_call" | custom-call | tf_op jit(solution)/shard_map/encode/pallas_call | solution.py:308
  123.6 67.2 %exchange_code.1 = (bf16[2,32,96,128]{3,2,1,0:T(8,128)(2,1)}, f32[2,96,128]{2,1,0:T(8,128)}) custom-call(f32[2,32,96,128]{3,2,1,0:T(8,128)} %bitcast.35, f32[2,96,128]{2,1,0:T(8,128)} %reshape.47.extra), custom_call_target="tpu_custom_call" | custom-call | tf_op jit(solution)/shard_map/exchange_code/pallas_call | solution.py:725
  190.8 20.4 %decode.1 = (bf16[64,128,256]{2,1,0:T(8,128)(2,1)}, bf16[64,128,256]{2,1,0:T(8,128)(2,1)}, bf16[32,384,192]{2,1,0:T(8,128)(2,1)}) custom-call(bf16[64,16,128]{2,1,0:T(8,128)(2,1)} %bitcast.32, bf16[64,96,128]{2,1,0:T(8,128)(2,1)} %bitcast.37, bf16[32,192,256]{2,1,0:T(8,128)(2,1)} %get-tuple-element.28.dec_hbm), custom_call_target="tpu_custom_call" | custom-call | tf_op jit(solution)/shard_map/decode/pallas_call | solution.py:368
  211.2 25.0 %errors.1 = (f32[64,96,128]{2,1,0:T(8,128)}, bf16[4,2,8,192,128]{4,3,2,1,0:T(8,128)(2,1)}) custom-call(bf16[64,16,128]{2,1,0:T(8,128)(2,1)} %bitcast.33, f32[8,256]{1,0:T(8,128)} %broadcast_in_dim.8.b_dec, bf16[64,128,256]{2,1,0:T(8,128)(2,1)} %bitcast.30, bf16[64,128,256]{2,1,0:T(8,128)(2,1)} %get-tuple-element.29.mine_hbm, ...), custom_call_target="tpu_custom_call" | custom-call | tf_op jit(solution)/shard_map/errors/pallas_call | solution.py:433
  236.2 75.3 %exchange_grad.1 = (bf16[2,32,96,128]{3,2,1,0:T(8,128)(2,1)}, bf16[16,192,128]{2,1,0:T(8,128)(2,1)}) custom-call(f32[2,32,96,128]{3,2,1,0:T(8,128)} %bitcast.34, f32[2,96,128]{2,1,0:T(8,128)} %get-tuple-element.33.extra, bf16[4,2,8,192,128]{4,3,2,1,0:T(8,128)(2,1)} %get-tuple-element.34.rest_0_), custom_call_target="tpu_custom_call" | custom-call | tf_op jit(solution)/shard_map/exchange_grad/pallas_call | solution.py:725
  311.4 10.1 %enc_grads.1 = (bf16[4,2,8,192,128]{4,3,2,1,0:T(8,128)(2,1)}, f32[32,8,128]{2,1,0:T(8,128)}) custom-call(bf16[64,96,128]{2,1,0:T(8,128)(2,1)} %bitcast.40, bf16[32,384,256]{2,1,0:T(8,128)(2,1)} %get-tuple-element.36.inputs_hbm), custom_call_target="tpu_custom_call" | custom-call | tf_op jit(solution)/shard_map/enc_grads/pallas_call | solution.py:470
  321.5 61.6 %deliver.1 = (bf16[16,192,128]{2,1,0:T(8,128)(2,1)}, bf16[16,192,128]{2,1,0:T(8,128)(2,1)}, f32[8,128]{1,0:T(8,128)}) custom-call(bf16[4,2,8,192,128]{4,3,2,1,0:T(8,128)(2,1)} %get-tuple-element.37.enc, bf16[16,192,128]{2,1,0:T(8,128)(2,1)} %get-tuple-element.38.dec_total, f32[32,8,128]{2,1,0:T(8,128)} %get-tuple-element.39.bias), custom_call_target="tpu_custom_call" | custom-call | tf_op jit(solution)/shard_map/deliver/pallas_call | solution.py:811
  383.2 0.8 add_bitcast_fusion
  384.0 0.7 slice_bitcast_fusion
  384.7 0.6 pad_maximum_fusion
  385.2 1.7 convert_bitcast_fusion
  387.0 1.3 copy.16
  388.3 1.3 copy.15

commit v2 on v1

--- a/solution.py
+++ b/solution.py
@@ -20,7 +20,7 @@
 LINES = NP * 3
 BIG = 60 * 1024 * 1024
 G_KIND = F32
-PARTS = 2
+PARTS = 3
 PART = LINES // PARTS
 
 
@@ -67,11 +67,55 @@
     lax.fori_loop(0, NP // 2, tile, 0)
 
 
-def spread_kernel(acts, info, w_enc, w_dec, acts_all, info_all, enc_all, dec_all,
-                  own, own_acts, acts_cut, enc_cut, dec_cut, local_sem, send_sem, acts_sem, info_sem, enc_sem, dec_sem,
-                  pair_sem, info_pair_sem, y_sem, far_sem, y_send):
+def brought(y):
+    return pl.ds(pl.multiple_of(y * 48, 16), 48)
+
+
+def bring(y, p, c, cut, ref, send, recv):
+    target = ref.at[p, brought(y), :]
+    sem = recv.at[lax.div(p, NZ)]
+    pltpu.make_async_copy(cut.at[p], target, sem).start()
+
+    def body(i, _):
+        q = shifted(p, i)
+        remote(cut.at[q], target, send, sem, (y, q * 2 + c)).start()
+        return 0
+
+    lax.fori_loop(1, NP, body, 0)
+
+
+def pass_own(y, p, c, ref, g, recv, y_send, y_sem):
+    part = ref.at[pl.ds(g * NZ, NZ), brought(y), :]
+    wait_bytes(part, recv.at[g])
+    for side, step in enumerate((1, NY - 1)):
+        remote(part, part, y_send.at[0], y_sem.at[side, g], (lax.rem(y + step, NY), p * 2 + c)).start()
+
+
+def pass_on(y, p, c, ref, g, y_send, y_sem, far_sem):
+    up, down = lax.rem(y + 1, NY), lax.rem(y + NY - 1, NY)
+    for side, (v, to) in enumerate(((down, up), (up, down))):
+        wait_bytes(ref.at[pl.ds(g * NZ, NZ), brought(v), :], y_sem.at[side, g])
+        part = ref.at[pl.ds(g * NZ + side * (NZ // 2), NZ // 2), brought(v), :]
+        remote(part, part, y_send.at[0], far_sem.at[side], (to, p * 2 + c)).start()
+
+
+def bring_end(cut, ref, send, y_send, far_sem):
+    for side in range(2):
+        wait_bytes(cut.at[pl.ds(0, NP // 2)], far_sem.at[side])
+    wait_bytes(ref.at[:, pl.ds(0, 144), :], y_send.at[0])
+    wait_bytes(cut.at[pl.ds(0, NP - 1)], send)
+
+
+def bring_sems():
+    dma = pltpu.SemaphoreType.DMA
+    return [dma((1,)), dma((NX,)), dma((1,)), dma((2, NX)), dma((2,))]
+
+
+def spread_kernel(acts, info, w_enc, w_dec, acts_all, info_all, enc_all, dec_cut,
+                  own, own_acts, acts_cut, enc_cut, local_sem, send_sem, acts_sem, info_sem,
+                  pair_sem, info_pair_sem, w_send, w_recv, y_send, y_sem, far_sem):
     y, p, c = place()
-    rows = pl.ds(pl.multiple_of(y * 48, 16), 48)
+    rows = brought(y)
     loads = [pltpu.make_async_copy(w_enc.at[rows, :], own.at[0], local_sem.at[0]),
              pltpu.make_async_copy(w_dec.at[rows, :], own.at[1], local_sem.at[1]),
              pltpu.make_async_copy(acts, own_acts, local_sem.at[2])]
@@ -89,78 +133,48 @@
         pl.semaphore_signal(barrier, inc=1, device_id=(lax.rem(y + j, NY), p * 2 + c), device_id_type=MESH)
     loads[0].wait()
     by_chip(own.at[0], enc_cut)
-    loads[1].wait()
-    by_chip(own.at[1], dec_cut)
     pl.semaphore_wait(barrier, NP - 1 + 1 + NY - 1)
 
     mine = lax.div(p, NZ)
-    pltpu.make_async_copy(enc_cut.at[p], enc_all.at[p, rows, :], enc_sem.at[mine]).start()
-    pltpu.make_async_copy(dec_cut.at[p], dec_all.at[p, rows, :], dec_sem.at[mine]).start()
     pltpu.make_async_copy(info, info_all.at[c, p], info_sem.at[0]).start()
 
-    def send_w(i, _):
-        q = shifted(p, i)
-        remote(enc_cut.at[q], enc_all.at[p, rows, :], send_sem.at[0], enc_sem.at[mine], (y, q * 2 + c)).start()
-        remote(dec_cut.at[q], dec_all.at[p, rows, :], send_sem.at[1], dec_sem.at[mine], (y, q * 2 + c)).start()
-        return 0
-
-    lax.fori_loop(1, NP, send_w, 0)
+    bring(y, p, c, enc_cut, enc_all, w_send.at[0], w_recv)
     loads[2].wait()
     by_chip(own_acts, acts_cut)
     pltpu.make_async_copy(acts_cut.at[p], acts_all.at[c, p], acts_sem.at[mine]).start()
 
     def send_a(i, _):
         q = shifted(p, i)
-        remote(info, info_all.at[c, p], send_sem.at[3], info_sem.at[0], (y, q * 2 + c)).start()
-        remote(acts_cut.at[q], acts_all.at[c, p], send_sem.at[2], acts_sem.at[mine], (y, q * 2 + c)).start()
+        remote(info, info_all.at[c, p], send_sem.at[1], info_sem.at[0], (y, q * 2 + c)).start()
+        remote(acts_cut.at[q], acts_all.at[c, p], send_sem.at[0], acts_sem.at[mine], (y, q * 2 + c)).start()
         return 0
 
     lax.fori_loop(1, NP, send_a, 0)
 
-    up, down = lax.rem(y + 1, NY), lax.rem(y + NY - 1, NY)
-    weights = ((enc_all, enc_sem, 0), (dec_all, dec_sem, 1))
-
-    def pass_own(g):
-        for ref, sem, n in weights:
-            part = ref.at[pl.ds(g * NZ, NZ), rows, :]
-            wait_bytes(part, sem.at[g])
-            for side, v in enumerate((up, down)):
-                remote(part, part, y_send.at[n], y_sem.at[n, side, g], (v, p * 2 + c)).start()
-
-    def pass_on(g):
-        for ref, _, n in weights:
-            for side, (v, to) in enumerate(((down, up), (up, down))):
-                theirs = pl.ds(pl.multiple_of(v * 48, 16), 48)
-                wait_bytes(ref.at[pl.ds(g * NZ, NZ), theirs, :], y_sem.at[n, side, g])
-                part = ref.at[pl.ds(g * NZ + side * (NZ // 2), NZ // 2), theirs, :]
-                remote(part, part, y_send.at[n], far_sem.at[n, side], (to, p * 2 + c)).start()
-
+    loads[1].wait()
+    by_chip(own.at[1], dec_cut)
     for i in range(NX + 1):
         if i < NX:
-            pass_own(lax.rem(mine - i + NX, NX))
+            pass_own(y, p, c, enc_all, lax.rem(mine - i + NX, NX), w_recv, y_send, y_sem)
         if i > 0:
-            pass_on(lax.rem(mine - i + 1 + NX, NX))
+            pass_on(y, p, c, enc_all, lax.rem(mine - i + 1 + NX, NX), y_send, y_sem, far_sem)
     pair = (y, p * 2 + 1 - c)
     wait_bytes(info_all.at[c], info_sem.at[0])
-    remote(info_all.at[c], info_all.at[c], send_sem.at[4], info_pair_sem.at[0], pair).start()
+    remote(info_all.at[c], info_all.at[c], send_sem.at[2], info_pair_sem.at[0], pair).start()
     for i in range(NX):
         g = lax.rem(mine - i + NX, NX)
         part = acts_all.at[c, pl.ds(g * NZ, NZ)]
         wait_bytes(part, acts_sem.at[g])
-        remote(part, part, send_sem.at[5], pair_sem.at[0], pair).start()
+        remote(part, part, send_sem.at[3], pair_sem.at[0], pair).start()
 
     wait_bytes(info_all.at[c], info_pair_sem.at[0])
     wait_bytes(acts_all.at[c], pair_sem.at[0])
-    for n, ref in ((0, enc_all), (1, dec_all)):
-        for side in range(2):
-            wait_bytes(enc_cut.at[pl.ds(0, NP // 2)], far_sem.at[n, side])
-        wait_bytes(ref.at[:, pl.ds(0, 144), :], y_send.at[n])
-        wait_bytes(enc_cut.at[pl.ds(0, NP - 1)], send_sem.at[n])
+    bring_end(enc_cut, enc_all, w_send.at[0], y_send, far_sem)
     most = pl.ds(0, NP - 1)
-    wait_bytes(acts_cut.at[most], send_sem.at[2])
-    wait_bytes(info_all.at[0, most], send_sem.at[3])
-    wait_bytes(info_all.at[0], send_sem.at[4])
-    wait_bytes(acts_cut, send_sem.at[5])
+    wait_bytes(acts_cut.at[most], send_sem.at[0])
+    wait_bytes(info_all.at[0, most], send_sem.at[1])
+    wait_bytes(info_all.at[0], send_sem.at[2])
+    wait_bytes(acts_cut, send_sem.at[3])
 
 
 def spread(acts, info, w_enc, w_dec):
@@ -171,14 +185,13 @@
             jax.ShapeDtypeStruct((2, NP, ROWS, DS), BF16),
             jax.ShapeDtypeStruct((2, NP, 16, 128), BF16),
             jax.ShapeDtypeStruct((NP, LOCAL, DS), BF16),
-            jax.ShapeDtypeStruct((NP, LOCAL, DS), BF16),
+            jax.ShapeDtypeStruct((NP, 48, DS), BF16),
         ),
         in_specs=[ANY] * 4,
-        out_specs=(ANY,) * 4,
+        out_specs=(ANY, ANY, ANY, VMEM),
         scratch_shapes=[pltpu.VMEM((2, 48, D), BF16), pltpu.VMEM((ROWS, D), BF16),
-                        pltpu.VMEM((NP, ROWS, DS), BF16), pltpu.VMEM((NP, 48, DS), BF16), pltpu.VMEM((NP, 48, DS), BF16),
-                        dma((3,)), dma((6,)), dma((NX,)), dma((1,)), dma((NX,)), dma((NX,)), dma((1,)), dma((1,)),
-                        dma((2, 2, NX)), dma((2, 2)), dma((2,))],
+                        pltpu.VMEM((NP, ROWS, DS), BF16), pltpu.VMEM((NP, 48, DS), BF16),
+                        dma((3,)), dma((4,)), dma((NX,)), dma((1,)), dma((1,)), dma((1,))] + bring_sems(),
         compiler_params=pltpu.CompilerParams(collective_id=0, has_side_effects=True, vmem_limit_bytes=BIG),
         name="spread",
     )(acts, info, w_enc, w_dec)
@@ -497,7 +510,7 @@
             pl.semaphore_signal(barrier, inc=1, device_id=at(v, h), device_id_type=MESH)
 
 
-MEET_PARTS = 2
+MEET_PARTS = 3
 MEET_ROWS = LOCAL // MEET_PARTS
 
 
@@ -571,8 +584,8 @@
 
 def exchange_kernel(forward, part, extra, *rest):
     if forward:
-        (out_all, slope_out, got, code, x_relay, x_merged, x_land, z_out, send_sem, xr_sem, xl_sem, recv_sem,
-         line_sem, x_sem, far_sem, back_sem) = rest
+        (dec_cut, out_all, slope_out, dec_all, got, code, x_relay, x_merged, x_land, z_out, send_sem, xr_sem, xl_sem, recv_sem,
+         line_sem, x_sem, far_sem, back_sem, w_send, w_recv, y_send, y_sem, w_far) = rest
     else:
         (dec, out_all, dec_total, got, code, x_relay, x_merged, x_land, z_out, send_sem, xr_sem, xl_sem, recv_sem,
          line_sem, x_sem, far_sem, back_sem, land, relay, merged, m_send, m_recv) = rest
@@ -586,17 +599,31 @@
     def in_line(i):
         return lax.rem(z + lax.rem(i, NZ), NZ), lax.rem(c + lax.div(i, NZ), 2)
 
-    def greet(i, _):
-        w, h = in_line(i)
-        pl.semaphore_signal(barrier, inc=1, device_id=(y, (x * NZ + w) * 2 + h), device_id_type=MESH)
-        return 0
-
-    lax.fori_loop(1, 2 * NZ, greet, 0)
-    for v in (right, left):
-        pl.semaphore_signal(barrier, inc=1, device_id=(y, (v * NZ + z) * 2 + c), device_id_type=MESH)
-    if not forward:
+    if forward:
+        def greet(i, _):
+            pl.semaphore_signal(barrier, inc=1, device_id=(y, shifted(p, i) * 2 + c), device_id_type=MESH)
+            return 0
+
+        def greet_other(w, _):
+            pl.semaphore_signal(barrier, inc=1, device_id=(y, (x * NZ + w) * 2 + 1 - c), device_id_type=MESH)
+            return 0
+
+        lax.fori_loop(1, NP, greet, 0)
+        lax.fori_loop(0, NZ, greet_other, 0)
+        for step in (1, NY - 1):
+            pl.semaphore_signal(barrier, inc=1, device_id=(lax.rem(y + step, NY), p * 2 + c), device_id_type=MESH)
+        pl.semaphore_wait(barrier, NP - 1 + NZ + 2)
+    else:
+        def greet(i, _):
+            w, h = in_line(i)
+            pl.semaphore_signal(barrier, inc=1, device_id=(y, (x * NZ + w) * 2 + h), device_id_type=MESH)
+            return 0
+
+        lax.fori_loop(1, 2 * NZ, greet, 0)
+        for v in (right, left):
+            pl.semaphore_signal(barrier, inc=1, device_id=(y, (v * NZ + z) * 2 + c), device_id_type=MESH)
         meet_greet(y, p, c, barrier)
-    pl.semaphore_wait(barrier, 17 if forward else 23)
+        pl.semaphore_wait(barrier, 23)
 
     def beside(v):
         return (y, (v * NZ + z) * 2 + c)
@@ -613,6 +640,8 @@
             remote(rows_of(far, k, n), cut(x_relay.at[k], n), send_sem.at[0], xr_sem.at[n, k], beside(to)).start()
         for to, _, k in ways:
             remote(rows_of(to, 1 - k, n), cut(x_land.at[k, 1 - k], n), send_sem.at[1], xl_sem.at[n], beside(to)).start()
+    if forward:
+        bring(y, p, c, dec_cut, dec_all, w_send.at[0], w_recv)
     for n in range(PARTS):
         own = pl.ds(n * PART, PART)
         for to, _, k in ways:
@@ -647,7 +676,10 @@
 
         lax.fori_loop(0, 2 * NZ, z_send, 0)
 
-    if not forward:
+    if forward:
+        for i in range(NX):
+            pass_own(y, p, c, dec_all, lax.rem(x - i + NX, NX), w_recv, y_send, y_sem)
+    else:
         meet_start(y, p, c, dec, land, relay, m_send, m_recv)
 
     for n in range(PARTS):
@@ -675,7 +707,10 @@
 
         lax.fori_loop(1, 2 * NZ, share, 0)
 
-    if not forward:
+    if forward:
+        for i in range(NX):
+            pass_on(y, p, c, dec_all, lax.rem(x - i + NX, NX), y_send, y_sem, w_far)
+    else:
         for n in range(MEET_PARTS):
             meet_merge(y, p, c, n, dec, land, relay, merged, m_send, m_recv)
 
@@ -711,7 +746,9 @@
     wait_bytes(out_all.at[0, pl.ds(0, 2 * NZ - 1)], back_sem.at[0])
     wait_bytes(out_all.at[0], back_sem.at[1])
     wait_bytes(out_all.at[0, pl.ds(0, 2 * NZ)], back_sem.at[2])
-    if not forward:
+    if forward:
+        bring_end(dec_cut, dec_all, w_send.at[0], y_send, w_far)
+    else:
         meet_end(land, relay, m_send)
 
 
@@ -720,19 +757,20 @@
     out = [jax.ShapeDtypeStruct((2, NP, LINES, 128), BF16)]
     if forward:
         out.append(jax.ShapeDtypeStruct((2, LINES, 128), F32))
+        out.append(jax.ShapeDtypeStruct((NP, LOCAL, DS), BF16))
     else:
         out.append(jax.ShapeDtypeStruct((16, LOCAL, 128), BF16))
     return pl.pallas_call(
         functools.partial(exchange_kernel, forward),
         out_shape=tuple(out),
         in_specs=[VMEM] * (2 + len(dec)),
-        out_specs=(VMEM,) * len(out),
+        out_specs=(VMEM, VMEM, ANY) if forward else (VMEM, VMEM),
         scratch_shapes=[pltpu.VMEM((2, NZ, LINES, 128), F32), pltpu.VMEM((2, LINES, 128), BF16),
                         pltpu.VMEM((2, NZ, LINES, 128), part.dtype), pltpu.VMEM((2, NZ, LINES, 128), part.dtype),
                         pltpu.VMEM((2, 2, NZ, LINES, 128), part.dtype), pltpu.VMEM((2, NZ, LINES, 128), F32),
                         dma((3,)), dma((PARTS, 2)), dma((PARTS,)), dma((PARTS,)), dma((PARTS,)), dma((PARTS, 2, 2)),
                         dma((PARTS, 2)), dma((3,))]
-        + ([] if forward else MEET_SCRATCH),
+        + (bring_sems() if forward else MEET_SCRATCH),
         compiler_params=pltpu.CompilerParams(
             collective_id=1 if forward else 2, has_side_effects=True, vmem_limit_bytes=BIG),
         name="exchange_code" if forward else "exchange_grad",
@@ -863,13 +901,13 @@
 def shards(acts, blocks, w_enc, b_enc, w_dec, b_dec):
     l = lax.axis_index("latent")
     p = l // 2
-    acts_all, info_all, enc_all, dec_all = spread(acts, info_of(blocks, b_enc), w_enc.T, w_dec)
+    acts_all, info_all, enc_all, dec_cut = spread(acts, info_of(blocks, b_enc), w_enc.T, w_dec)
     acts_all = acts_all.reshape(64, ROWS, DS)
     info_all = info_all.reshape(64, 16, 128)
     inputs, part = encode(info_all, acts_all, enc_all)
     bias = info_all.astype(F32)
     bias = (bias[:, 4:7] + bias[:, 7:10] + bias[:, 10:13]).reshape(2, LINES, 128)
-    codes, slope = exchange(True, part, bias)
+    codes, slope, dec_all = exchange(True, part, bias, dec_cut)
     recon, other, wide = decode(info_all, codes.reshape(64, LINES, 128), dec_all)
     my_b_dec = lax.dynamic_slice(b_dec.reshape(NY, D // NY), (0, pair_of(p) * 128 + p // NZ % 2 * 64), (NY, 64))
     my_b_dec = jnp.broadcast_to(my_b_dec.reshape(1, DS), (8, DS))

time: 390 us -> 381 us (0.977)
  Pallas kernels: 379 us -> 370 us
    pallas_call x1, Pallas kernels: 99 us -> 82.4 us  [spread(): pl.pallas_call(spread_kernel, out_shape=(jax.ShapeDtypeStruct((2, NP, ROW...]
    pallas_call x2, Pallas kernels: 142 us -> 152 us  [exchange(): pl.pallas_call(functools.partial(exchange_kernel, forward), out_shape=tup...]
where the time goes in v2:
time: 381 us
  Pallas kernels  370 us (97%)
  local copies, waits for them, and re-layouts  5.56 us (1%)
  other arithmetic  4.19 us (1%)
    pallas_call x2, Pallas kernels, exchange(): pl.pallas_call(functools.partial(exchange_kernel, forward), out_shape=tup...  152 us
    pallas_call x1, Pallas kernels, spread(): pl.pallas_call(spread_kernel, out_shape=(jax.ShapeDtypeStruct((2, NP, ROW...  82.4 us
    pallas_call x1, Pallas kernels, deliver(): pl.pallas_call(deliver_kernel, out_shape=(jax.ShapeDtypeStruct((16, LOCAL...  58.5 us
    pallas_call x1, Pallas kernels, errors_of(): pl.pallas_call(errors_kernel, out_shape=(jax.ShapeDtypeStruct((64, LINES,...  25 us
    pallas_call x1, Pallas kernels, decode(): pl.pallas_call(decode_kernel, out_shape=(jax.ShapeDtypeStruct((64, ROWS,...  21.8 us
    pallas_call x1, Pallas kernels, encode(): pl.pallas_call(encode_kernel, out_shape=(jax.ShapeDtypeStruct((NP, 384, D...  19.2 us
    pallas_call x1, Pallas kernels, enc_grads(): pl.pallas_call(enc_grads_kernel, out_shape=(jax.ShapeDtypeStruct((NY, 2,...  10.1 us

profile of v2, /device:TPU:1, one launch (start us, length us, event | category | flops | bytes accessed | tf_op | source)
XLA Modules:
  0.0 381.0 jit_solution(3049735390600018539)
XLA Ops:
  0.7 1.4 info.1
  2.1 0.8 reshape.44
  2.9 0.1 constant_dynamic-slice_fusion
  3.0 0.1 broadcast_in_dim.7
  3.0 0.6 broadcast_in_dim.8.b_dec
  3.7 82.4 %spread.1 = (bf16[2,32,128,256]{3,2,1,0:T(8,128)(2,1)}, bf16[2,32,16,128]{3,2,1,0:T(8,128)(2,1)}, bf16[32,192,256]{2,1,0:T(8,128)(2,1)}, bf16[32,48,256]{2,1,0:T(8,128)(2,1)}) custom-call(bf16[128,8192]{1,0:T(8,128)(2,1)} %acts.1, bf16[16,128]{1,0:T(8,128)(2,1)} %info.1, bf16[192,8192]{1,0:T(8,128)(2,1)} %bitcast.35, bf16[192,8192]{1,0:T(8,128)(2,1)} %w_dec.1), custom_call_target="tpu_custom_call" | custom-call | tf_op jit(solution)/shard_map/spread/pallas_call | solution.py:182
  86.1 1.0 bitcast_convert_fusion
  87.0 0.1 slice_add_fusion
  87.1 0.7 reshape.47.extra
  87.8 19.2 %encode.1 = (bf16[32,384,256]{2,1,0:T(8,128)(2,1)}, f32[64,96,128]{2,1,0:T(8,128)}) custom-call(bf16[64,16,128]{2,1,0:T(8,128)(2,1)} %bitcast.31, bf16[64,128,256]{2,1,0:T(8,128)(2,1)} %bitcast.29, bf16[32,192,256]{2,1,0:T(8,128)(2,1)} %get-tuple-element.26.enc_hbm), custom_call_target="tpu_custom_call" | custom-call | tf_op jit(solution)/shard_map/encode/pallas_call | solution.py:321
  107.0 77.7 %exchange_code.1 = (bf16[2,32,96,128]{3,2,1,0:T(8,128)(2,1)}, f32[2,96,128]{2,1,0:T(8,128)}, bf16[32,192,256]{2,1,0:T(8,128)(2,1)}) custom-call(f32[2,32,96,128]{3,2,1,0:T(8,128)} %bitcast.36, f32[2,96,128]{2,1,0:T(8,128)} %reshape.47.extra, bf16[32,48,256]{2,1,0:T(8,128)(2,1)} %get-tuple-element.28.rest_0_), custom_call_target="tpu_custom_call" | custom-call | tf_op jit(solution)/shard_map/exchange_code/pallas_call | solution.py:763
  184.7 21.8 %decode.1 = (bf16[64,128,256]{2,1,0:T(8,128)(2,1)}, bf16[64,128,256]{2,1,0:T(8,128)(2,1)}, bf16[32,384,192]{2,1,0:T(8,128)(2,1)}) custom-call(bf16[64,16,128]{2,1,0:T(8,128)(2,1)} %bitcast.32, bf16[64,96,128]{2,1,0:T(8,128)(2,1)} %bitcast.37, bf16[32,192,256]{2,1,0:T(8,128)(2,1)} %get-tuple-element.30.dec_hbm), custom_call_target="tpu_custom_call" | custom-call | tf_op jit(solution)/shard_map/decode/pallas_call | solution.py:381
  206.5 25.0 %errors.1 = (f32[64,96,128]{2,1,0:T(8,128)}, bf16[4,2,8,192,128]{4,3,2,1,0:T(8,128)(2,1)}) custom-call(bf16[64,16,128]{2,1,0:T(8,128)(2,1)} %bitcast.33, f32[8,256]{1,0:T(8,128)} %broadcast_in_dim.8.b_dec, bf16[64,128,256]{2,1,0:T(8,128)(2,1)} %bitcast.30, bf16[64,128,256]{2,1,0:T(8,128)(2,1)} %get-tuple-element.31.mine_hbm, ...), custom_call_target="tpu_custom_call" | custom-call | tf_op jit(solution)/shard_map/errors/pallas_call | solution.py:446
  231.5 74.5 %exchange_grad.1 = (bf16[2,32,96,128]{3,2,1,0:T(8,128)(2,1)}, bf16[16,192,128]{2,1,0:T(8,128)(2,1)}) custom-call(f32[2,32,96,128]{3,2,1,0:T(8,128)} %bitcast.34, f32[2,96,128]{2,1,0:T(8,128)} %get-tuple-element.35.extra, bf16[4,2,8,192,128]{4,3,2,1,0:T(8,128)(2,1)} %get-tuple-element.36.rest_0_), custom_call_target="tpu_custom_call" | custom-call | tf_op jit(solution)/shard_map/exchange_grad/pallas_call | solution.py:763
  306.0 10.1 %enc_grads.1 = (bf16[4,2,8,192,128]{4,3,2,1,0:T(8,128)(2,1)}, f32[32,8,128]{2,1,0:T(8,128)}) custom-call(bf16[64,96,128]{2,1,0:T(8,128)(2,1)} %bitcast.40, bf16[32,384,256]{2,1,0:T(8,128)(2,1)} %get-tuple-element.38.inputs_hbm), custom_call_target="tpu_custom_call" | custom-call | tf_op jit(solution)/shard_map/enc_grads/pallas_call | solution.py:483
  316.0 58.5 %deliver.1 = (bf16[16,192,128]{2,1,0:T(8,128)(2,1)}, bf16[16,192,128]{2,1,0:T(8,128)(2,1)}, f32[8,128]{1,0:T(8,128)}) custom-call(bf16[4,2,8,192,128]{4,3,2,1,0:T(8,128)(2,1)} %get-tuple-element.39.enc, bf16[16,192,128]{2,1,0:T(8,128)(2,1)} %get-tuple-element.40.dec_total, f32[32,8,128]{2,1,0:T(8,128)} %get-tuple-element.41.bias), custom_call_target="tpu_custom_call" | custom-call | tf_op jit(solution)/shard_map/deliver/pallas_call | solution.py:849
  374.5 0.8 add_bitcast_fusion
  375.4 0.7 slice_bitcast_fusion
  376.1 0.6 pad_maximum_fusion
  376.6 1.7 convert_bitcast_fusion
  378.4 1.3 copy.16
  379.7 1.3 copy.15

commit v3 on v2

--- a/solution.py
+++ b/solution.py
@@ -582,6 +582,10 @@
     return 0.5 * (1.0 + lax.erf(v * 0.7071067811865476)) + v * jnp.exp(-0.5 * v * v) * 0.3989422804014327
 
 
+def beside_part(n):
+    return range(n * NX // PARTS, (n + 1) * NX // PARTS)
+
+
 def exchange_kernel(forward, part, extra, *rest):
     if forward:
         (dec_cut, out_all, slope_out, dec_all, got, code, x_relay, x_merged, x_land, z_out, send_sem, xr_sem, xl_sem, recv_sem,
@@ -675,11 +679,11 @@
             return 0
 
         lax.fori_loop(0, 2 * NZ, z_send, 0)
-
-    if forward:
-        for i in range(NX):
-            pass_own(y, p, c, dec_all, lax.rem(x - i + NX, NX), w_recv, y_send, y_sem)
-    else:
+        if forward:
+            for i in beside_part(n):
+                pass_own(y, p, c, dec_all, lax.rem(x - i + NX, NX), w_recv, y_send, y_sem)
+
+    if not forward:
         meet_start(y, p, c, dec, land, relay, m_send, m_recv)
 
     for n in range(PARTS):
@@ -706,11 +710,11 @@
             return 0
 
         lax.fori_loop(1, 2 * NZ, share, 0)
-
-    if forward:
-        for i in range(NX):
-            pass_on(y, p, c, dec_all, lax.rem(x - i + NX, NX), y_send, y_sem, w_far)
-    else:
+        if forward:
+            for i in beside_part(n):
+                pass_on(y, p, c, dec_all, lax.rem(x - i + NX, NX), y_send, y_sem, w_far)
+
+    if not forward:
         for n in range(MEET_PARTS):
             meet_merge(y, p, c, n, dec, land, relay, merged, m_send, m_recv)
 
@@ -832,7 +836,8 @@
 
         lax.fori_loop(0, 8, enc_owner, 0)
     wait_bytes(bias_y, b_recv.at[0])
-    bias_out[...] = bias_y[0] + bias_y[1] + bias_y[2] + bias_y[3]
+    total = bias_y[0] + bias_y[1] + bias_y[2] + bias_y[3]
+    bias_out[...] = jnp.concatenate([total[0:1], total[1:2, 0:BW] + total[1:2, BW:128]], axis=1)
     wait_bytes(bias_y.at[pl.ds(0, NY - 1)], b_send.at[0])
     meet_end(land, relay, m_send)
     for n in range(2):
@@ -851,7 +856,7 @@
         out_shape=(
             jax.ShapeDtypeStruct((16, LOCAL, 128), BF16),
             jax.ShapeDtypeStruct((16, LOCAL, 128), BF16),
-            jax.ShapeDtypeStruct((8, 128), F32),
+            jax.ShapeDtypeStruct((1, LOCAL), F32),
         ),
         in_specs=[VMEM, VMEM, ANY],
         out_specs=(ANY, ANY, VMEM),
@@ -915,7 +920,7 @@
     g_all, dec_total = exchange(False, g_part, slope, dec)
     enc, bias_sum = enc_grads(g_all.reshape(64, LINES, 128), inputs)
     enc_tiles, dec_tiles, lines = deliver(enc, dec_total, bias_sum)
-    grad_b_enc = jnp.concatenate([lines[0], lines[1, 0:64] + lines[1, 64:128]])
+    grad_b_enc = lines.reshape(LOCAL)
 
     def whole(tiles):
         return tiles.transpose(1, 0, 2).reshape(LOCAL, D // NY).astype(F32)

time: 381 us -> 379 us (level)
  no operation moved by 1% of the time
where the time goes in v3:
time: 379 us; the launch traced here: 378 us
  Pallas kernels  369 us (97%)
  local copies, waits for them, and re-layouts  5.44 us (1%)
    pallas_call x2, Pallas kernels, exchange(): pl.pallas_call(functools.partial(exchange_kernel, forward), out_shape=tup...  153 us
    pallas_call x1, Pallas kernels, spread(): pl.pallas_call(spread_kernel, out_shape=(jax.ShapeDtypeStruct((2, NP, ROW...  82.4 us
    pallas_call x1, Pallas kernels, deliver(): pl.pallas_call(deliver_kernel, out_shape=(jax.ShapeDtypeStruct((16, LOCAL...  58.6 us
    pallas_call x1, Pallas kernels, errors_of(): pl.pallas_call(errors_kernel, out_shape=(jax.ShapeDtypeStruct((64, LINES,...  25 us
    pallas_call x1, Pallas kernels, encode(): pl.pallas_call(encode_kernel, out_shape=(jax.ShapeDtypeStruct((NP, 384, D...  19.2 us
    pallas_call x1, Pallas kernels, decode(): pl.pallas_call(decode_kernel, out_shape=(jax.ShapeDtypeStruct((64, ROWS,...  18.9 us
    pallas_call x1, Pallas kernels, enc_grads(): pl.pallas_call(enc_grads_kernel, out_shape=(jax.ShapeDtypeStruct((NY, 2,...  10.1 us

profile of v3, /device:TPU:1, one launch (start us, length us, event | category | flops | bytes accessed | tf_op | source)
XLA Modules:
  0.0 378.0 jit_solution(14467506477893706388)
XLA Ops:
  0.7 1.4 info.1
  2.1 0.8 reshape.46
  2.9 0.1 constant_dynamic-slice_fusion
  3.0 0.1 broadcast_in_dim.7
  3.0 0.6 broadcast_in_dim.8.b_dec
  3.7 82.4 %spread.1 = (bf16[2,32,128,256]{3,2,1,0:T(8,128)(2,1)}, bf16[2,32,16,128]{3,2,1,0:T(8,128)(2,1)}, bf16[32,192,256]{2,1,0:T(8,128)(2,1)}, bf16[32,48,256]{2,1,0:T(8,128)(2,1)}) custom-call(bf16[128,8192]{1,0:T(8,128)(2,1)} %acts.1, bf16[16,128]{1,0:T(8,128)(2,1)} %info.1, bf16[192,8192]{1,0:T(8,128)(2,1)} %bitcast.32, bf16[192,8192]{1,0:T(8,128)(2,1)} %w_dec.1), custom_call_target="tpu_custom_call" | custom-call | tf_op jit(solution)/shard_map/spread/pallas_call | solution.py:182
  86.0 1.0 bitcast_convert_fusion
  87.0 0.1 slice_add_fusion
  87.1 0.7 reshape.49.extra
  87.8 19.2 %encode.1 = (bf16[32,384,256]{2,1,0:T(8,128)(2,1)}, f32[64,96,128]{2,1,0:T(8,128)}) custom-call(bf16[64,16,128]{2,1,0:T(8,128)(2,1)} %bitcast.28, bf16[64,128,256]{2,1,0:T(8,128)(2,1)} %bitcast.26, bf16[32,192,256]{2,1,0:T(8,128)(2,1)} %get-tuple-element.26.enc_hbm), custom_call_target="tpu_custom_call" | custom-call | tf_op jit(solution)/shard_map/encode/pallas_call | solution.py:321
  107.0 77.9 %exchange_code.1 = (bf16[2,32,96,128]{3,2,1,0:T(8,128)(2,1)}, f32[2,96,128]{2,1,0:T(8,128)}, bf16[32,192,256]{2,1,0:T(8,128)(2,1)}) custom-call(f32[2,32,96,128]{3,2,1,0:T(8,128)} %bitcast.33, f32[2,96,128]{2,1,0:T(8,128)} %reshape.49.extra, bf16[32,48,256]{2,1,0:T(8,128)(2,1)} %get-tuple-element.28.rest_0_), custom_call_target="tpu_custom_call" | custom-call | tf_op jit(solution)/shard_map/exchange_code/pallas_call | solution.py:767
  184.9 18.9 %decode.1 = (bf16[64,128,256]{2,1,0:T(8,128)(2,1)}, bf16[64,128,256]{2,1,0:T(8,128)(2,1)}, bf16[32,384,192]{2,1,0:T(8,128)(2,1)}) custom-call(bf16[64,16,128]{2,1,0:T(8,128)(2,1)} %bitcast.29, bf16[64,96,128]{2,1,0:T(8,128)(2,1)} %bitcast.34, bf16[32,192,256]{2,1,0:T(8,128)(2,1)} %get-tuple-element.30.dec_hbm), custom_call_target="tpu_custom_call" | custom-call | tf_op jit(solution)/shard_map/decode/pallas_call | solution.py:381
  203.8 25.0 %errors.1 = (f32[64,96,128]{2,1,0:T(8,128)}, bf16[4,2,8,192,128]{4,3,2,1,0:T(8,128)(2,1)}) custom-call(bf16[64,16,128]{2,1,0:T(8,128)(2,1)} %bitcast.30, f32[8,256]{1,0:T(8,128)} %broadcast_in_dim.8.b_dec, bf16[64,128,256]{2,1,0:T(8,128)(2,1)} %bitcast.27, bf16[64,128,256]{2,1,0:T(8,128)(2,1)} %get-tuple-element.31.mine_hbm, ...), custom_call_target="tpu_custom_call" | custom-call | tf_op jit(solution)/shard_map/errors/pallas_call | solution.py:446
  228.8 75.5 %exchange_grad.1 = (bf16[2,32,96,128]{3,2,1,0:T(8,128)(2,1)}, bf16[16,192,128]{2,1,0:T(8,128)(2,1)}) custom-call(f32[2,32,96,128]{3,2,1,0:T(8,128)} %bitcast.31, f32[2,96,128]{2,1,0:T(8,128)} %get-tuple-element.35.extra, bf16[4,2,8,192,128]{4,3,2,1,0:T(8,128)(2,1)} %get-tuple-element.36.rest_0_), custom_call_target="tpu_custom_call" | custom-call | tf_op jit(solution)/shard_map/exchange_grad/pallas_call | solution.py:767
  304.3 10.1 %enc_grads.1 = (bf16[4,2,8,192,128]{4,3,2,1,0:T(8,128)(2,1)}, f32[32,8,128]{2,1,0:T(8,128)}) custom-call(bf16[64,96,128]{2,1,0:T(8,128)(2,1)} %bitcast.37, bf16[32,384,256]{2,1,0:T(8,128)(2,1)} %get-tuple-element.38.inputs_hbm), custom_call_target="tpu_custom_call" | custom-call | tf_op jit(solution)/shard_map/enc_grads/pallas_call | solution.py:483
  314.4 58.6 %deliver.1 = (bf16[16,192,128]{2,1,0:T(8,128)(2,1)}, bf16[16,192,128]{2,1,0:T(8,128)(2,1)}, f32[1,192]{1,0:T(1,128)}) custom-call(bf16[4,2,8,192,128]{4,3,2,1,0:T(8,128)(2,1)} %get-tuple-element.39.enc, bf16[16,192,128]{2,1,0:T(8,128)(2,1)} %get-tuple-element.40.dec_total, f32[32,8,128]{2,1,0:T(8,128)} %get-tuple-element.41.bias), custom_call_target="tpu_custom_call" | custom-call | tf_op jit(solution)/shard_map/deliver/pallas_call | solution.py:854
  373.1 1.7 convert_bitcast_fusion
  374.8 0.0 copy-start
  374.8 1.3 copy.16
  376.1 1.3 copy.15
  377.5 0.0 copy-done
  377.5 0.6 copy.18
Async XLA Ops:
  374.8 2.7 copy-start
